TPU v7x, 256 devices: a whole 4x4x8 slice. The times are simulated.
256 devices in a mesh: dp: 8 (over z), cand: 32 (over y, x, core).
Axes of the slice: x: 4, y: 4, z: 8, core: 2. Of those that a mesh axis runs over, the one named last changes fastest.
Arguments:
- queries: bfloat16 [128, 32, 32, 128], P('dp', 'cand'), may hold values from -1 to 1, as said below
- passages: bfloat16 [128, 8, 256, 128], P('cand'), may hold values from -1 to 1, as said below
- cand_ids: int32 [128, 2], P('dp'), may hold values from 0 to 127, as said below
- pos_index: int32 [128, 32], P('dp'), may hold values from 0 to 15
Outputs:
- losses: float32 [128, 32], P('dp', 'cand')
- query_grads: float32 [128, 32, 32, 128], P('dp', 'cand')
- passage_grads: float32 [128, 8, 256, 128], P('cand', 'dp')
Inputs may be any that keep to these rules, and one draw needn't show every extreme that they name: `queries`: every token vector has unit length. `passages`: every token vector has unit length. `cand_ids`: block k is stored on index k // 4 of cand. Within the 16 rows of one index of dp, at most 4 of the entries name blocks stored on one index of cand, and in every such group of rows some index of cand is named by exactly 4 entries. The two entries of a row may be equal.
All inputs are finite; a program needn't handle non-finite values.
Results may differ from a plain program's by a relative error of at most 0.0003.
Values may be sent and summed in bfloat16 or wider, within the bound.
A program may use at most 128 MiB of HBM per device.

v0:
```python
import jax
import jax.numpy as jnp
from jax import lax
from jax.sharding import PartitionSpec as P

softness = 0.05
loss_scale = 32.0


def slot_tiles(query_block, passage_block):
    query_flat = query_block.reshape(-1, query_block.shape[-1])
    passage_flat = passage_block.reshape(-1, passage_block.shape[-1])
    similar = lax.dot_general(
        query_flat, passage_flat, (((1,), (1,)), ((), ())), preferred_element_type=jnp.float32
    )
    exponent = jnp.exp(similar / softness).reshape(
        query_flat.shape[0], passage_block.shape[0], passage_block.shape[1]
    )
    totals = jnp.sum(exponent, -1)
    weights = exponent / totals[:, :, None]
    soft_max = softness * jnp.log(totals)
    scores = jnp.sum(
        soft_max.reshape(query_block.shape[0], query_block.shape[1], passage_block.shape[0]), 1
    )
    return (scores, weights, query_flat, passage_flat)


def tile_grads(weights, grad_tile, query_flat, passage_flat, tokens):
    expanded = jnp.repeat(grad_tile, tokens, axis=0)
    sim_grad = (weights * expanded[:, :, None]).reshape(query_flat.shape[0], passage_flat.shape[0])
    query_wide = query_flat.astype(jnp.float32)
    passage_wide = passage_flat.astype(jnp.float32)
    query_grad = jnp.dot(
        sim_grad, passage_wide, precision=lax.Precision.HIGHEST, preferred_element_type=jnp.float32
    )
    passage_grad = lax.dot_general(
        sim_grad,
        query_wide,
        (((0,), (0,)), ((), ())),
        precision=lax.Precision.HIGHEST,
        preferred_element_type=jnp.float32,
    )
    return (query_grad, passage_grad)


def on_device(queries, passages, cand_ids, pos_index):
    cand_count = lax.axis_size("cand")
    my_index = lax.axis_index("cand")
    row_blocks = queries.shape[0]
    share = queries.shape[1]
    tokens = queries.shape[2]
    width = queries.shape[3]
    blocks_here = passages.shape[0]
    per_block = passages.shape[1]
    passage_len = passages.shape[2]
    query_count = share * cand_count
    requests = 2 * row_blocks
    capacity = 4 * ((requests + cand_count - 1) // cand_count)
    zero_index = jnp.int32(0)
    flat_ids = cand_ids.reshape(-1)
    owners = flat_ids // blocks_here
    is_mine = owners[None, :] == jnp.arange(cand_count, dtype=jnp.int32)[:, None]
    places = jnp.cumsum(is_mine.astype(jnp.int32), 1) - 1
    slot_hit = is_mine[:, :, None] & (
        places[:, :, None] == jnp.arange(capacity, dtype=jnp.int32)[None, None, :]
    )
    slot_requests = jnp.sum(
        jnp.where(slot_hit, jnp.arange(requests, dtype=jnp.int32)[None, :, None], 0), 1
    )
    owner_counts = jnp.sum(is_mine.astype(jnp.int32), 1)
    slot_valid = jnp.arange(capacity, dtype=jnp.int32)[None, :] < owner_counts[:, None]
    my_requests = slot_requests[my_index]
    my_valid = slot_valid[my_index].astype(jnp.float32)
    whole_rows = lax.all_gather(queries, "cand", axis=1, tiled=True)

    def fetch_block(block_row):
        return whole_rows[block_row]

    first_slot = 0

    def slot_parts(slot):
        request = my_requests[slot]
        block_row = request // 2
        column = request % 2 * per_block
        local_block = flat_ids[request] % blocks_here
        tiles = slot_tiles(fetch_block(block_row), passages[local_block])
        return (block_row, column, local_block, tiles)

    def forward_slot(slot, logit_table):
        block_row, column, local_block, tiles = slot_parts(slot)
        current = lax.dynamic_slice(
            logit_table, (block_row, zero_index, column), (1, query_count, per_block)
        )
        return lax.dynamic_update_slice(
            logit_table, current + my_valid[slot] * tiles[0][None], (block_row, zero_index, column)
        )

    logit_table = jnp.zeros((row_blocks, query_count, 2 * per_block), jnp.float32)
    logit_table = lax.fori_loop(first_slot, capacity, forward_slot, logit_table)
    logits = lax.psum(logit_table, "cand")
    log_total = jnp.log(jnp.sum(jnp.exp(logits), -1))
    onehot = (
        jnp.arange(2 * per_block, dtype=jnp.int32)[None, None, :] == pos_index[:, :, None]
    ).astype(jnp.float32)
    row_losses = log_total - jnp.sum(logits * onehot, -1)
    losses = lax.dynamic_slice_in_dim(row_losses, my_index * share, share, 1)
    dlogit = loss_scale * (jnp.exp(logits - log_total[:, :, None]) - onehot)

    def backward_slot(slot, state):
        passage_acc, query_acc = state
        block_row, column, local_block, tiles = slot_parts(slot)
        scores, weights, query_flat, passage_flat = tiles
        grad_tile = (
            lax.dynamic_slice(dlogit, (block_row, zero_index, column), (1, query_count, per_block))[
                0
            ]
            * my_valid[slot]
        )
        query_grad, passage_grad = tile_grads(weights, grad_tile, query_flat, passage_flat, tokens)
        current_query = lax.dynamic_slice_in_dim(query_acc, block_row, 1, 0)
        query_acc = lax.dynamic_update_slice_in_dim(
            query_acc, current_query + query_grad[None], block_row, 0
        )
        current_passage = lax.dynamic_slice_in_dim(passage_acc, local_block, 1, 0)
        passage_acc = lax.dynamic_update_slice_in_dim(
            passage_acc, current_passage + passage_grad[None], local_block, 0
        )
        return (passage_acc, query_acc)

    passage_acc = jnp.zeros((blocks_here, per_block * passage_len, width), jnp.float32)
    query_acc = jnp.zeros((row_blocks, query_count * tokens, width), jnp.float32)
    passage_acc, query_acc = lax.fori_loop(
        first_slot, capacity, backward_slot, (passage_acc, query_acc)
    )
    query_grads = lax.psum_scatter(
        query_acc.reshape(row_blocks, query_count, tokens, width),
        "cand",
        scatter_dimension=1,
        tiled=True,
    )
    passage_grads = lax.psum_scatter(
        passage_acc.reshape(blocks_here, per_block, passage_len, width),
        "dp",
        scatter_dimension=1,
        tiled=True,
    )
    return (losses, query_grads, passage_grads)


def solution(mesh):
    in_specs = (
        P("dp", "cand", None, None),
        P("cand", None, None, None),
        P("dp", None),
        P("dp", None),
    )
    out_specs = (P("dp", "cand"), P("dp", "cand", None, None), P("cand", "dp", None, None))
    return jax.shard_map(
        on_device, mesh=mesh, in_specs=in_specs, out_specs=out_specs, check_vma=False
    )
```

profile of v0, /device:TPU:1, one launch (start us, length us, event | category | flops | bytes accessed | tf_op | source)
XLA Modules:
  0.0 814.6 jit_solution(3861843050267787062)
XLA Ops:
  10.7 58.2 %all-gather.2.cloned.1.call-done = bf16[16,32,32,128]{3,2,1,0:T(8,128)(2,1)} async-done(((bf16[16,1,32,128]{3,2,1,0:T(8,128)(2,1)}), bf16[16,32,32,128]{3,2,1,0:T(8,128)(2,1)}) %all-gather.2.cloned.1.call-update) | async-done | bytes 4194320 | tf_op jit(solution)/shard_map/all_gather | solution.py:74
  69.0 97.2 %while.34 = (s32[]{:T(128)}, f32[16,32,16]{2,1,0:T(8,128)S(1)}, s32[4]{0:T(128)S(1)}, f32[4]{0:T(128)S(1)}, bf16[16,32,32,128]{3,2,1,0:T(8,128)(2,1)}, /*index=5...) while((s32[]{:T(128)}, f32[16,32,16]{2,1,0:T(8,128)S(1)}, ...), condition=%wide.region_6.7_spmd, body=%wide.region_3.6_spmd.sunk | while | flops 541073728 | bytes 36184728 | solution.py:99
  79.4 7.3 copy.47
  103.8 7.3 copy.47
  128.0 7.3 copy.47
  152.3 7.3 copy.47
  166.2 122.3 %psum.7 = f32[16,32,16]{2,1,0:T(8,128)S(1)} all-reduce(f32[16,32,16]{2,1,0:T(8,128)S(1)} %get-tuple-element.468), channel_id=1, replica_groups=mesh['dp'=8,'cand'=32] {'cand'}, use_global_device_ids=true, to_apply=%region_7.8 | all-reduce | flops 8192 | bytes 65536 | tf_op jit(solution)/shard_map/psum | solution.py:100
  296.6 264.9 %while.35 = (s32[]{:T(128)}, f32[4,2048,128]{2,1,0:T(8,128)}, f32[16,1024,128]{2,1,0:T(8,128)}, s32[4]{0:T(128)S(1)}, s32[32]{0:T(128)S(1)}, /*index=5*/bf16[16,...) while((s32[]{:T(128)}, f32[4,2048,128]{2,1,0:T(8,128)}, ...), condition=%wide.region_12.13_spmd, body=%wide.region_10.12_spmd.sunk | while | flops 6986015232 | bytes 140578464 | solution.py:132
  325.0 7.3 copy.50
  335.6 7.3 copy.51
  347.5 7.3 copy.52
  354.8 7.3 divide_multiply_fusion.2
  362.1 9.1 %fusion.39 = f32[4,2048,128]{2,1,0:T(8,128)} fusion(f32[4,2048,128]{2,1,0:T(8,128)} %get-tuple-element.711, s32[]{:T(128)S(6)} %select_n.260, f32[1024,2048]{1,0:T(8,128)S(1)} %divide_multiply_fusion.2, bf16[1024,128]{1,0:T(8,128)(2,1)S(1)} %bitcast.139), kind=kOutput, calls=%fused_computation.10.clone.1 | convolution fusion | flops 3221487616 | bytes 10747908 | tf_op jit(solution)/shard_map/while/body/eval_jaxpr/dot_general | solution.py:36
  371.2 5.8 fusion.40
  386.5 7.3 copy.50
  397.1 7.3 copy.51
  409.0 7.3 copy.52
  416.3 7.3 divide_multiply_fusion.2
  423.6 9.1 %fusion.39 = f32[4,2048,128]{2,1,0:T(8,128)} fusion(f32[4,2048,128]{2,1,0:T(8,128)} %get-tuple-element.711, s32[]{:T(128)S(6)} %select_n.260, f32[1024,2048]{1,0:T(8,128)S(1)} %divide_multiply_fusion.2, bf16[1024,128]{1,0:T(8,128)(2,1)S(1)} %bitcast.139), kind=kOutput, calls=%fused_computation.10.clone.1 | convolution fusion | flops 3221487616 | bytes 10747908 | tf_op jit(solution)/shard_map/while/body/eval_jaxpr/dot_general | solution.py:36
  432.7 5.8 fusion.40
  447.9 7.3 copy.50
  458.5 7.3 copy.51
  470.4 7.3 copy.52
  477.7 7.3 divide_multiply_fusion.2
  485.0 9.2 %fusion.39 = f32[4,2048,128]{2,1,0:T(8,128)} fusion(f32[4,2048,128]{2,1,0:T(8,128)} %get-tuple-element.711, s32[]{:T(128)S(6)} %select_n.260, f32[1024,2048]{1,0:T(8,128)S(1)} %divide_multiply_fusion.2, bf16[1024,128]{1,0:T(8,128)(2,1)S(1)} %bitcast.139), kind=kOutput, calls=%fused_computation.10.clone.1 | convolution fusion | flops 3221487616 | bytes 10747908 | tf_op jit(solution)/shard_map/while/body/eval_jaxpr/dot_general | solution.py:36
  509.4 7.3 copy.50
  520.0 7.3 copy.51
  531.9 7.3 copy.52
  539.2 7.3 divide_multiply_fusion.2
  546.5 9.1 %fusion.39 = f32[4,2048,128]{2,1,0:T(8,128)} fusion(f32[4,2048,128]{2,1,0:T(8,128)} %get-tuple-element.711, s32[]{:T(128)S(6)} %select_n.260, f32[1024,2048]{1,0:T(8,128)S(1)} %divide_multiply_fusion.2, bf16[1024,128]{1,0:T(8,128)(2,1)S(1)} %bitcast.139), kind=kOutput, calls=%fused_computation.10.clone.1 | convolution fusion | flops 3221487616 | bytes 10747908 | tf_op jit(solution)/shard_map/while/body/eval_jaxpr/dot_general | solution.py:36
  564.1 129.9 %all-reduce.5.cloned.1.call-done = f32[16,32,32,128]{3,2,1,0:T(8,128)} async-done(((f32[16,32,32,128]{3,2,1,0:T(8,128)}), f32[16,32,32,128]{3,2,1,0:T(8,128)}) %all-reduce.5.cloned.1.call-update) | async-done | bytes 8388624
  696.3 108.9 %all-reduce.7.cloned.1.call-done = f32[4,8,256,128]{3,2,1,0:T(8,128)} async-done(((f32[4,8,256,128]{3,2,1,0:T(8,128)}), f32[4,8,256,128]{3,2,1,0:T(8,128)}) %all-reduce.7.cloned.1.call-update) | async-done | bytes 4194320
  (139 shorter events, 120.9 us)
Async XLA Ops:
  7.2 61.8 %all-gather.2.cloned.1.call-start = ((), (), s32[]{:S(2)}) async-start(), calls=%async_computation | async-start | bytes 4325376 | tf_op jit(solution)/shard_map/all_gather | solution.py:74
  7.9 686.1 %all-reduce.5.cloned.1.call-start = ((), (), s32[]{:S(2)}) async-start(), calls=%async_computation.1 | async-start | bytes 16777216
  69.0 219.5 %copy-start.2 = (s32[16,32]{1,0:T(8,128)S(1)}, s32[16,32]{1,0:T(8,128)}, u32[]{:S(2)}) copy-start(s32[16,32]{1,0:T(8,128)} %param.11) | copy-start | bytes 6148
  289.4 0.6 copy-start
  561.4 0.8 copy-start.5
  561.4 1.4 copy-start.4
  561.4 2.0 copy-start.1
  561.4 2.0 copy-start.3
  561.5 243.8 %all-reduce.7.cloned.1.call-start = ((), (), s32[]{:S(2)}) async-start(), calls=%async_computation.2 | async-start | bytes 8388608
Sparse Core Ops, SparseCore 0:
  10.5 58.4 all-gather.1
  561.6 132.3 all-reduce.4
  696.5 108.6 all-reduce.6
where the time goes:
time: 824 us; the launch traced here: 815 us
  waiting for transfers between devices  298 us (36%)
  local copies, waits for them, and re-layouts  170 us (21%)
  blocking collectives  122 us (15%)
  other arithmetic  74 us (9%)
  matrix products  69.9 us (8%)
  loops' own time  65.5 us (8%)
  between operations  14.2 us (2%)
    unnamed x5, waiting for transfers between devices  240 us
    psum x1, blocking collectives, on_device(): logits = lax.psum(logit_table, 'cand')  122 us
    while x20, local copies, waits for them, and re-layouts  118 us
    all_gather x1, waiting for transfers between devices, on_device(): whole_rows = lax.all_gather(queries, 'cand', axis=1, tiled=True)  58.2 us
    another operation x1, loops' own time, on_device(): lax.fori_loop(first_slot, capacity, backward_slot, (passage_acc, query_acc))  41.8 us
    dot_general x4, matrix products, tile_grads(): lax.dot_general(sim_grad, query_wide, (((0,), (0,)), ((), ())), precision...  36.6 us
    mul x4, other arithmetic, tile_grads(): weights * expanded[:, :, None]  29 us
    another operation x1, loops' own time, on_device(): logit_table = lax.fori_loop(first_slot, capacity, forward_slot, logit_table)  23.7 us
  transfers between devices with their start and end apart: 3, of which 3 were waited for; matrix products, arithmetic and copies ran while one was open for 1% of the time, Pallas kernels for 0%

commit v1 on v0

v1 whole, which is shorter than its diff:
```python
import functools
import math

import jax
import jax.numpy as jnp
from jax import lax
from jax.experimental import pallas as pl
from jax.experimental.pallas import tpu as pltpu
from jax.sharding import PartitionSpec as P

softness = 0.05
loss_scale = 32.0
to_exp2 = math.log2(math.e) / softness
MESH = pl.DeviceIdType.MESH
HIGHEST = lax.Precision.HIGHEST
LANES = 128


def tables_kernel(blocks_here, cap, ids_ref, request_ref, place_ref, counts_ref):
    def clear_count(owner, _):
        counts_ref[owner] = 0
        return 0

    def clear_request(place, _):
        request_ref[place] = -1
        return 0

    def put(request, _):
        owner = ids_ref[request] // blocks_here
        slot = counts_ref[owner]
        counts_ref[owner] = slot + 1
        request_ref[owner * cap + slot] = request
        place_ref[request] = owner * cap + slot
        return 0

    lax.fori_loop(0, counts_ref.shape[0], clear_count, 0)
    lax.fori_loop(0, request_ref.shape[0], clear_request, 0)
    lax.fori_loop(0, ids_ref.shape[0], put, 0)


def main_kernel(
    rows,
    ring,
    cap,
    request_ref,
    place_ref,
    ids_ref,
    q_ref,
    p_ref,
    pos_ref,
    loss_ref,
    query_out,
    passage_out,
    q_send,
    q_slot,
    e_buf,
    totals,
    scores,
    grad_t,
    grad_slot,
    grad_back,
    acc,
    z_buf,
    send_sem,
    q_sem,
    score_sem,
    back_sem,
    z_send_sem,
    z_recv_sem,
):
    row_blocks, tokens, width = q_ref.shape
    blocks_here, per_block, passage_len, _ = p_ref.shape
    flat = rows * tokens
    me = lax.axis_index("cand")
    plane = lax.axis_index("dp")
    half_blocks = blocks_here // 2

    def peer_of(offset):
        return lax.rem(me + offset, rows)

    barrier = pltpu.get_barrier_semaphore()

    def greet(offset, _):
        pl.semaphore_signal(
            barrier, inc=1, device_id={"cand": peer_of(offset)}, device_id_type=MESH
        )
        return 0

    lax.fori_loop(1, rows, greet, 0)
    up, down = lax.rem(plane + 1, ring), lax.rem(plane + ring - 1, ring)
    for neighbour in (up, down):
        pl.semaphore_signal(barrier, inc=1, device_id={"dp": neighbour}, device_id_type=MESH)

    def fill(owner, _):
        for slot in range(cap):
            request = jnp.maximum(request_ref[owner * cap + slot], 0)
            q_send[slot, owner] = q_ref[request // 2]
        return 0

    lax.fori_loop(0, rows, fill, 0)
    my_rows = pl.ds(pl.multiple_of(me * tokens, tokens), tokens)
    pl.semaphore_wait(barrier, rows - 1 + 2)

    def q_copy(slot, peer):
        return pltpu.make_async_remote_copy(
            src_ref=q_send.at[slot, peer],
            dst_ref=q_slot.at[slot, my_rows],
            send_sem=send_sem.at[0],
            recv_sem=q_sem.at[slot],
            device_id={"cand": peer},
            device_id_type=MESH,
        )

    for slot in range(cap):

        def send_queries(offset, _, slot=slot):
            q_copy(slot, peer_of(offset)).start()
            return 0

        lax.fori_loop(1, rows, send_queries, 0)
        q_slot[slot, my_rows] = q_send[slot, me]

    head = pl.ds(0, flat - tokens)
    lane = lax.broadcasted_iota(jnp.int32, (flat, LANES), 1)
    query_of = lax.broadcasted_iota(jnp.int32, (flat, LANES), 0) // tokens
    my_scores = jnp.zeros((per_block, LANES), jnp.float32)

    def my_request(slot):
        return request_ref[me * cap + slot]

    def my_block(slot):
        return ids_ref[jnp.maximum(my_request(slot), 0)] % blocks_here

    def forward(slot, my_scores):
        pltpu.make_async_copy(q_slot.at[slot, head], q_slot.at[slot, head], q_sem.at[slot]).wait()
        block = my_block(slot)

        def candidate(c, _):
            similar = lax.dot_general(
                p_ref[block, c],
                q_slot[slot],
                (((1,), (1,)), ((), ())),
                preferred_element_type=jnp.float32,
            )
            exponent = jnp.exp2(similar * to_exp2)
            e_buf[slot, c] = exponent
            totals[slot, pl.ds(c, 1)] = jnp.sum(exponent, 0, keepdims=True)
            return 0

        lax.fori_loop(0, per_block, candidate, 0)
        soft_max = softness * jnp.log(totals[slot])
        place = (query_of + slot * rows == lane).astype(jnp.float32)
        return my_scores + jnp.dot(
            soft_max, place, precision=HIGHEST, preferred_element_type=jnp.float32
        )

    my_scores = lax.fori_loop(0, cap, forward, my_scores)
    scores[me] = my_scores

    def score_copy(peer):
        return pltpu.make_async_remote_copy(
            src_ref=scores.at[me],
            dst_ref=scores.at[me],
            send_sem=send_sem.at[1],
            recv_sem=score_sem,
            device_id={"cand": peer},
            device_id_type=MESH,
        )

    def send_scores(offset, _):
        score_copy(peer_of(offset)).start()
        return 0

    lax.fori_loop(1, rows, send_scores, 0)
    others = pl.ds(0, rows - 1)
    pltpu.make_async_copy(scores.at[others], scores.at[others], score_sem).wait()

    lane_in = lax.broadcasted_iota(jnp.int32, (LANES, rows), 0)
    query_in = lax.broadcasted_iota(jnp.int32, (LANES, rows), 1)

    def scores_of(place):
        pick = (lane_in == query_in + (place % cap) * rows).astype(jnp.float32)
        return jnp.dot(
            scores[place // cap], pick, precision=HIGHEST, preferred_element_type=jnp.float32
        )

    column = lax.broadcasted_iota(jnp.int32, (per_block, rows), 0)
    spread = (
        lax.broadcasted_iota(jnp.int32, (rows, flat), 1) // tokens
        == lax.broadcasted_iota(jnp.int32, (rows, flat), 0)
    ).astype(jnp.float32)

    def factors(slot, _):
        request = my_request(slot)
        valid = jnp.where(request >= 0, loss_scale, 0.0)
        request = jnp.maximum(request, 0)
        block_row, half = request // 2, request % 2
        mine = scores_of(me * cap + slot)
        other = scores_of(place_ref[block_row * 2 + 1 - half])
        log_total = jnp.log(
            jnp.sum(jnp.exp(mine), 0, keepdims=True) + jnp.sum(jnp.exp(other), 0, keepdims=True)
        )
        onehot = (column + half * per_block == pos_ref[block_row]).astype(jnp.float32)
        dlogit = valid * (jnp.exp(mine - log_total) - onehot)
        wide = jnp.dot(dlogit, spread, precision=HIGHEST, preferred_element_type=jnp.float32)
        totals[slot] = wide / totals[slot]
        return 0

    lax.fori_loop(0, cap, factors, 0)

    plus, minus = ring // 2, ring - 1 - ring // 2
    chains = []
    first = 0
    for half, sign, length in ((0, 1, plus), (0, -1, minus), (1, 1, minus), (1, -1, plus)):
        chains.append((half, sign, length, first))
        first += length

    def plane_at(offset):
        return lax.rem(plane + offset + ring, ring)

    def z_copy(chain, step):
        half, sign, length, first = chain
        if step == 0:
            source = acc.at[plane_at(sign * length), pl.ds(half * half_blocks, half_blocks)]
        else:
            source = z_buf.at[first + step - 1]
        return pltpu.make_async_remote_copy(
            src_ref=source,
            dst_ref=z_buf.at[first + step],
            send_sem=z_send_sem.at[first + step],
            recv_sem=z_recv_sem.at[first + step],
            device_id={"dp": up if sign > 0 else down},
            device_id_type=MESH,
        )

    grad_t[...] = jnp.zeros_like(grad_t)

    def gradients(step, _):
        near = jnp.where(step % 2 == 1, ring // 2 - (step + 1) // 2, step // 2 + ring // 2)
        c = lax.rem(plane + near, ring)
        acc[c] = jnp.zeros(acc.shape[1:], jnp.float32)

        def one_slot(slot, _):
            block = my_block(slot)
            passage = p_ref[block, c]
            queries = q_slot[slot]
            sim_grad = e_buf[slot, c] * totals[slot, pl.ds(c, 1)]
            high = sim_grad.astype(jnp.bfloat16)
            low = (sim_grad - high.astype(jnp.float32)).astype(jnp.bfloat16)
            passage_grad = jnp.dot(high, queries, preferred_element_type=jnp.float32) + jnp.dot(
                low, queries, preferred_element_type=jnp.float32
            )
            for local in range(blocks_here):
                chosen = jnp.where(block == local, 1.0, 0.0)
                acc[c, local] += chosen * passage_grad
            across = (((0,), (0,)), ((), ()))
            grad_t[slot] += lax.dot_general(
                passage, high, across, preferred_element_type=jnp.float32
            ) + lax.dot_general(passage, low, across, preferred_element_type=jnp.float32)
            return 0

        lax.fori_loop(0, cap, one_slot, 0)
        for chain in chains:
            half, sign, length, first = chain
            if length:
                at = [k for k in range(ring) if order[k] % ring == (sign * length) % ring][0]

                @pl.when(step == at)
                def _(chain=chain):
                    z_copy(chain, 0).start()

        return 0

    order = [
        ring // 2 - (k + 1) // 2 if k % 2 == 1 else k // 2 + ring // 2 for k in range(ring)
    ]
    lax.fori_loop(0, per_block, gradients, 0)

    def back_copy(peer):
        peer_rows = pl.ds(pl.multiple_of(peer * tokens, tokens), tokens)
        return pltpu.make_async_remote_copy(
            src_ref=grad_slot.at[:, peer_rows],
            dst_ref=grad_back.at[me],
            send_sem=send_sem.at[2],
            recv_sem=back_sem,
            device_id={"cand": peer},
            device_id_type=MESH,
        )

    def turn(slot, _):
        grad_slot[slot] = grad_t[slot].T
        return 0

    lax.fori_loop(0, cap, turn, 0)

    def send_back(offset, _):
        back_copy(peer_of(offset)).start()
        return 0

    lax.fori_loop(1, rows, send_back, 0)
    grad_back[me] = grad_slot[:, my_rows]

    for step in range(1, plus):
        for chain in chains:
            half, sign, length, first = chain
            if step < length:
                z_copy(chain, step - 1).wait_recv()
                target = plane_at(sign * (length - step))
                z_buf[first + step - 1] += acc[target, pl.ds(half * half_blocks, half_blocks)]
                z_copy(chain, step).start()

    def loss_row(block_row, _):
        first = scores_of(place_ref[2 * block_row])
        second = scores_of(place_ref[2 * block_row + 1])
        log_total = jnp.log(
            jnp.sum(jnp.exp(first), 0, keepdims=True) + jnp.sum(jnp.exp(second), 0, keepdims=True)
        )
        positive = pos_ref[block_row]
        chosen = jnp.sum(jnp.where(column == positive, first, 0.0), 0, keepdims=True) + jnp.sum(
            jnp.where(column + per_block == positive, second, 0.0), 0, keepdims=True
        )
        here = lax.broadcasted_iota(jnp.int32, (1, rows), 1) == me
        loss = jnp.sum(jnp.where(here, log_total - chosen, 0.0), 1, keepdims=True)
        loss_ref[pl.ds(block_row, 1)] = loss
        return 0

    lax.fori_loop(0, row_blocks, loss_row, 0)

    pltpu.make_async_copy(grad_back.at[others], grad_back.at[others], back_sem).wait()

    def add_pair(block_row, _):
        one, two = place_ref[2 * block_row], place_ref[2 * block_row + 1]
        query_out[block_row] = grad_back[one // cap, one % cap] + grad_back[two // cap, two % cap]
        return 0

    lax.fori_loop(0, row_blocks, add_pair, 0)

    for half in range(2):
        here = pl.ds(half * half_blocks, half_blocks)
        result = acc[plane, here]
        for chain in chains:
            if chain[0] == half and chain[2]:
                z_copy(chain, chain[2] - 1).wait_recv()
                result = result + z_buf[chain[3] + chain[2] - 1]
        passage_out[here] = result

    for slot in range(cap):
        pltpu.make_async_copy(q_slot.at[slot, head], q_slot.at[slot, head], send_sem.at[0]).wait()
    pltpu.make_async_copy(scores.at[others], scores.at[others], send_sem.at[1]).wait()
    pltpu.make_async_copy(grad_back.at[others], grad_back.at[others], send_sem.at[2]).wait()
    for chain in chains:
        for step in range(chain[2]):
            z_copy(chain, step).wait_send()


def on_device(rows, ring, queries, passages, cand_ids, pos_index):
    row_blocks, _, tokens, width = queries.shape
    blocks_here, per_block, passage_len, _ = passages.shape
    requests = 2 * row_blocks
    cap = 4 * ((requests + rows - 1) // rows)
    flat = rows * tokens
    smem = pl.BlockSpec(memory_space=pltpu.SMEM)
    vmem = pl.BlockSpec(memory_space=pltpu.VMEM)
    flat_ids = cand_ids.reshape(-1)
    request_at, place_of = pl.pallas_call(
        functools.partial(tables_kernel, blocks_here, cap),
        out_shape=(
            jax.ShapeDtypeStruct((rows * cap,), jnp.int32),
            jax.ShapeDtypeStruct((requests,), jnp.int32),
        ),
        in_specs=[smem],
        out_specs=(smem, smem),
        scratch_shapes=[pltpu.SMEM((rows,), jnp.int32)],
        name="tables",
    )(flat_ids)
    half_blocks = blocks_here // 2
    hops = 2 * (ring - 1)
    f32, bf16 = jnp.float32, jnp.bfloat16
    losses, query_grads, passage_grads = pl.pallas_call(
        functools.partial(main_kernel, rows, ring, cap),
        out_shape=(
            jax.ShapeDtypeStruct((row_blocks, 1), f32),
            jax.ShapeDtypeStruct((row_blocks, tokens, width), f32),
            jax.ShapeDtypeStruct((blocks_here, passage_len, width), f32),
        ),
        in_specs=[smem] * 3 + [vmem] * 3,
        out_specs=(vmem, vmem, vmem),
        scratch_shapes=[
            pltpu.VMEM((cap, rows, tokens, width), bf16),
            pltpu.VMEM((cap, flat, width), bf16),
            pltpu.VMEM((cap, per_block, passage_len, flat), f32),
            pltpu.VMEM((cap, per_block, flat), f32),
            pltpu.VMEM((rows, per_block, LANES), f32),
            pltpu.VMEM((cap, width, flat), f32),
            pltpu.VMEM((cap, flat, width), f32),
            pltpu.VMEM((rows, cap, tokens, width), f32),
            pltpu.VMEM((per_block, blocks_here, passage_len, width), f32),
            pltpu.VMEM((hops, half_blocks, passage_len, width), f32),
            pltpu.SemaphoreType.DMA((3,)),
            pltpu.SemaphoreType.DMA((cap,)),
            pltpu.SemaphoreType.DMA,
            pltpu.SemaphoreType.DMA,
            pltpu.SemaphoreType.DMA((hops,)),
            pltpu.SemaphoreType.DMA((hops,)),
        ],
        compiler_params=pltpu.CompilerParams(
            collective_id=0, has_side_effects=True, vmem_limit_bytes=60 * 1024 * 1024
        ),
        name="late_interaction",
    )(
        request_at,
        place_of,
        flat_ids,
        queries.reshape(row_blocks, tokens, width),
        passages,
        pos_index.reshape(row_blocks, 1, -1),
    )
    return (losses, query_grads[:, None], passage_grads[:, None])


def solution(mesh):
    in_specs = (
        P("dp", "cand", None, None),
        P("cand", None, None, None),
        P("dp", None),
        P("dp", None),
    )
    out_specs = (P("dp", "cand"), P("dp", "cand", None, None), P("cand", "dp", None, None))
    return jax.shard_map(
        functools.partial(on_device, mesh.shape["cand"], mesh.shape["dp"]),
        mesh=mesh,
        in_specs=in_specs,
        out_specs=out_specs,
        check_vma=False,
    )
```

time: 824 us -> 100 us (0.12); the launches traced: 815 us -> 100 us
  waiting for transfers between devices: 298 us -> 0 us
  local copies, waits for them, and re-layouts: 170 us -> 6.18 us
  blocking collectives: 122 us -> 0 us
  Pallas kernels: 0 us -> 93.2 us
  other arithmetic: 74 us -> 0 us
  matrix products: 69.9 us -> 0 us
  loops' own time: 65.5 us -> 0 us
  between operations: 14.2 us -> 0.65 us
    unnamed x5 -> x0, waiting for transfers between devices: 240 us -> none
    psum x1 -> x0, blocking collectives: 122 us -> none  [on_device(): logits = lax.psum(logit_table, 'cand')]
    while x20 -> x0, local copies, waits for them, and re-layouts: 118 us -> none
    pallas_call x0 -> x2, Pallas kernels: none -> 93.2 us  [the longest x1 90.4 us: on_device(): pl.pallas_call(functools.partial(main_kernel, rows, ring, cap), out_shape...]
    dot_general x16 -> x0, matrix products: 69.9 us -> none  [the longest x4 36.6 us: tile_grads(): lax.dot_general(sim_grad, query_wide, (((0,), (0,)), ((), ())), precision...]
    another operation x2 -> x0, loops' own time: 65.5 us -> none  [the longest x1 41.8 us: on_device(): lax.fori_loop(first_slot, capacity, backward_slot, (passage_acc, query_acc))]
    all_gather x1 -> x0, waiting for transfers between devices: 58.2 us -> none  [on_device(): whole_rows = lax.all_gather(queries, 'cand', axis=1, tiled=True)]
    mul x13 -> x0, other arithmetic: 32.2 us -> none  [the longest x4 29 us: tile_grads(): weights * expanded[:, :, None]]
  transfers between devices with their start and end apart: 3 -> 0, of which waited for: 3 -> 0; matrix products, arithmetic and copies ran while one was open for 1% -> 0% of each run, Pallas kernels for 0% -> 0%
where the time goes in v1:
time: 100 us
  Pallas kernels  93.2 us (93%)
  local copies, waits for them, and re-layouts  6.18 us (6%)
    pallas_call x1, Pallas kernels, on_device(): pl.pallas_call(functools.partial(main_kernel, rows, ring, cap), out_shape...  90.4 us
    unnamed x4, local copies, waits for them, and re-layouts  5.58 us
    pallas_call x1, Pallas kernels, on_device(): pl.pallas_call(functools.partial(tables_kernel, blocks_here, cap), out_sh...  2.8 us

profile of v1, /device:TPU:1, one launch (start us, length us, event | category | flops | bytes accessed | tf_op | source)
XLA Modules:
  0.0 100.1 jit_solution(4576276060455490473)
XLA Ops:
  0.6 0.8 copy.11
  1.4 0.6 reshape.15.ids_ref
  2.0 2.8 %tables.1 = (s32[128]{0:T(128)}, s32[32]{0:T(128)}) custom-call(s32[32]{0:T(128)} %reshape.15.ids_ref), custom_call_target="tpu_custom_call" | custom-call | tf_op jit(solution)/shard_map/tables/pallas_call | solution.py:365
  4.8 90.4 %late_interaction.1 = (f32[16,1]{1,0:T(8,128)}, f32[16,32,128]{2,1,0:T(8,128)}, f32[4,256,128]{2,1,0:T(8,128)}) custom-call(s32[128]{0:T(128)} %get-tuple-element.8.request_ref, s32[32]{0:T(128)} %get-tuple-element.9.place_ref, s32[32]{0:T(128)} %reshape.15.ids_ref, bf16[16,32,128]{2,1,0:T(8,128)(2,1)} %bitcast.10, bf16[4,8,256,128]{3,2,1,0:T(8,128)(2,1)} %p_ref.1, ...), custom_call_target="tpu_custom_call" | custom-call | tf_op jit(solution)/shard_map/late_interaction/pallas_call | solution.py:379
  95.2 1.3 %copy.12 = f32[16,1]{0,1:T(1,128)} copy(f32[16,1]{1,0:T(8,128)} %get-tuple-element.16) | data formatting | bytes 128
  96.5 1.7 %copy.17 = f32[16,1,32,128]{3,2,1,0:T(8,128)} copy(f32[16,1,32,128]{3,2,1,0:T(8,128)} %bitcast.9) | data formatting | bytes 524288
  98.2 1.9 %copy.18 = f32[4,1,256,128]{3,2,1,0:T(8,128)} copy(f32[4,1,256,128]{3,2,1,0:T(8,128)} %bitcast.8) | data formatting | bytes 1048576

commit v2 on v1

v2 whole, which is shorter than its diff:
```python
import functools
import math

import jax
import jax.numpy as jnp
from jax import lax
from jax.experimental import pallas as pl
from jax.experimental.pallas import tpu as pltpu
from jax.sharding import PartitionSpec as P

softness = 0.05
loss_scale = 32.0
to_exp2 = math.log2(math.e) / softness
MESH = pl.DeviceIdType.MESH
HIGHEST = lax.Precision.HIGHEST
LANES = 128
CODE_ROWS = 16
SCALE_STEPS = 256.0
TOP = 32700.0
TINY = 1e-30
GROUP = 32
CHUNK = 256


def to_codes(values):
    top = jnp.maximum(jnp.max(jnp.abs(values), 1), TINY)
    scale_code = jnp.ceil(SCALE_STEPS * (jnp.log2(top) - math.log2(TOP)))
    inverse = jnp.exp2(scale_code * (-1.0 / SCALE_STEPS))
    codes = jnp.round(values * inverse[:, None, :]).astype(jnp.int32).astype(jnp.int16)
    return codes, scale_code


def scale_of(scale_code):
    return jnp.exp2(scale_code * (1.0 / SCALE_STEPS))


def fill_tables(blocks_here, cap, ids_ref, table):
    count = ids_ref.shape[0] * ids_ref.shape[1]
    columns = ids_ref.shape[1]
    along = lax.broadcasted_iota(jnp.int32, (count, LANES), 1)
    down = lax.broadcasted_iota(jnp.int32, (count, LANES), 0)
    owner_along = jnp.full((count, LANES), -1, jnp.int32)
    owner_down = jnp.full((count, LANES), -1, jnp.int32)
    for request in range(count):
        owner = ids_ref[request // columns, request % columns] // blocks_here
        owner_along = jnp.where(along == request, owner, owner_along)
        owner_down = jnp.where(down == request, owner, owner_down)
    same = owner_along == owner_down
    rank_along = jnp.sum((same & (down < along)).astype(jnp.int32), 0, keepdims=True)
    place_along = owner_along[:1] * cap + rank_along
    rank_down = jnp.sum((same & (along < down)).astype(jnp.int32), 1, keepdims=True)
    here = owner_down * cap + rank_down == along
    request_along = jnp.sum(jnp.where(here, down + 1, 0), 0, keepdims=True) - 1
    row = lax.broadcasted_iota(jnp.int32, table.shape, 0)
    table[...] = jnp.where(row == 0, request_along, place_along)


def main_kernel(
    rows,
    ring,
    cap,
    ids_ref,
    q_ref,
    p_ref,
    pos_ref,
    loss_ref,
    query_out,
    passage_out,
    table,
    table_s,
    q_send,
    q_slot,
    q_turned,
    p_turned,
    high,
    low,
    totals,
    scores,
    grad_t,
    back_scales,
    back_out,
    back_in,
    acc,
    z_out,
    z_in,
    table_sem,
    send_sem,
    q_sem,
    score_sem,
    back_sem,
    z_send_sem,
    z_recv_sem,
):
    row_blocks, tokens, width = q_ref.shape
    blocks_here, per_block, passage_len, _ = p_ref.shape
    flat = rows * tokens
    chunk = min(CHUNK, flat)
    me = lax.axis_index("cand")
    plane = lax.axis_index("dp")
    half_blocks = blocks_here // 2
    groups = half_blocks * passage_len // GROUP
    values_here = half_blocks * passage_len
    tiles = tokens // CODE_ROWS

    def peer_of(offset):
        return lax.rem(me + offset, rows)

    barrier = pltpu.get_barrier_semaphore()

    def greet(offset, _):
        pl.semaphore_signal(
            barrier, inc=1, device_id={"cand": peer_of(offset)}, device_id_type=MESH
        )
        return 0

    lax.fori_loop(1, rows, greet, 0)
    up, down = lax.rem(plane + 1, ring), lax.rem(plane + ring - 1, ring)
    for neighbour in (up, down):
        pl.semaphore_signal(barrier, inc=1, device_id={"dp": neighbour}, device_id_type=MESH)

    fill_tables(blocks_here, cap, ids_ref, table)
    to_scalars = pltpu.make_async_copy(table, table_s, table_sem)
    to_scalars.start()
    to_scalars.wait()

    def request_at(place):
        return table_s[0, place]

    def place_of(request):
        return table_s[1, request]

    def fill(owner, _):
        for slot in range(cap):
            request = jnp.maximum(request_at(owner * cap + slot), 0)
            q_send[slot, owner] = q_ref[request // 2]
        return 0

    lax.fori_loop(0, rows, fill, 0)
    my_rows = pl.ds(pl.multiple_of(me * tokens, tokens), tokens)
    pl.semaphore_wait(barrier, rows - 1 + 2)

    def q_copy(slot, peer):
        return pltpu.make_async_remote_copy(
            src_ref=q_send.at[slot, peer],
            dst_ref=q_slot.at[slot, my_rows],
            send_sem=send_sem.at[0],
            recv_sem=q_sem.at[slot],
            device_id={"cand": peer},
            device_id_type=MESH,
        )

    for slot in range(cap):

        def send_queries(offset, _, slot=slot):
            q_copy(slot, peer_of(offset)).start()
            return 0

        lax.fori_loop(1, rows, send_queries, 0)
        q_slot[slot, my_rows] = q_send[slot, me]

    def turn_passage(c, _):
        for block in range(blocks_here):
            p_turned[block, c] = p_ref[block, c].T
        return 0

    lax.fori_loop(0, per_block, turn_passage, 0)

    head = pl.ds(0, flat - tokens)
    lane = lax.broadcasted_iota(jnp.int32, (flat, LANES), 1)
    query_of = lax.broadcasted_iota(jnp.int32, (flat, LANES), 0) // tokens
    my_scores = jnp.zeros((per_block, LANES), jnp.float32)

    def my_request(slot):
        return request_at(me * cap + slot)

    def my_block(slot):
        request = jnp.maximum(my_request(slot), 0)
        return ids_ref[request // 2, request % 2] % blocks_here

    def forward(slot, my_scores):
        pltpu.make_async_copy(q_slot.at[slot, head], q_slot.at[slot, head], q_sem.at[slot]).wait()
        block = my_block(slot)
        q_turned[slot] = q_slot[slot].T

        def candidate(c, _):
            passage = p_ref[block, c]
            for start in range(0, flat, chunk):
                here = pl.ds(start, chunk)
                similar = jnp.dot(
                    passage, q_turned[slot, :, here], preferred_element_type=jnp.float32
                )
                exponent = jnp.exp2(similar * to_exp2)
                rounded = exponent.astype(jnp.bfloat16)
                high[slot, c, :, here] = rounded
                low[slot, c, :, here] = (exponent - rounded.astype(jnp.float32)).astype(
                    jnp.bfloat16
                )
                totals[slot, pl.ds(c, 1), here] = jnp.sum(exponent, 0, keepdims=True)
            return 0

        lax.fori_loop(0, per_block, candidate, 0)
        soft_max = softness * jnp.log(totals[slot])
        place = (query_of + slot * rows == lane).astype(jnp.float32)
        return my_scores + jnp.dot(
            soft_max, place, precision=HIGHEST, preferred_element_type=jnp.float32
        )

    my_scores = lax.fori_loop(0, cap, forward, my_scores)
    scores[me] = my_scores

    def send_scores(offset, _):
        pltpu.make_async_remote_copy(
            src_ref=scores.at[me],
            dst_ref=scores.at[me],
            send_sem=send_sem.at[1],
            recv_sem=score_sem,
            device_id={"cand": peer_of(offset)},
            device_id_type=MESH,
        ).start()
        return 0

    lax.fori_loop(1, rows, send_scores, 0)
    others = pl.ds(0, rows - 1)
    pltpu.make_async_copy(scores.at[others], scores.at[others], score_sem).wait()

    lane_in = lax.broadcasted_iota(jnp.int32, (LANES, rows), 0)
    query_in = lax.broadcasted_iota(jnp.int32, (LANES, rows), 1)

    def scores_of(place):
        pick = (lane_in == query_in + (place % cap) * rows).astype(jnp.float32)
        return jnp.dot(
            scores[place // cap], pick, precision=HIGHEST, preferred_element_type=jnp.float32
        )

    column = lax.broadcasted_iota(jnp.int32, (per_block, rows), 0)
    spread = (
        lax.broadcasted_iota(jnp.int32, (rows, flat), 1) // tokens
        == lax.broadcasted_iota(jnp.int32, (rows, flat), 0)
    ).astype(jnp.float32)

    position_row = lax.broadcasted_iota(jnp.int32, pos_ref.shape, 0)

    def positives(block_row):
        return jnp.sum(jnp.where(position_row == block_row, pos_ref[...], 0), 0, keepdims=True)

    def factors(slot, _):
        request = my_request(slot)
        valid = jnp.where(request >= 0, loss_scale, 0.0)
        request = jnp.maximum(request, 0)
        block_row, half = request // 2, request % 2
        mine = scores_of(me * cap + slot)
        other = scores_of(place_of(block_row * 2 + 1 - half))
        log_total = jnp.log(
            jnp.sum(jnp.exp(mine), 0, keepdims=True) + jnp.sum(jnp.exp(other), 0, keepdims=True)
        )
        onehot = (column + half * per_block == positives(block_row)).astype(jnp.float32)
        dlogit = valid * (jnp.exp(mine - log_total) - onehot)
        wide = jnp.dot(dlogit, spread, precision=HIGHEST, preferred_element_type=jnp.float32)
        totals[slot] = wide / totals[slot]
        return 0

    lax.fori_loop(0, cap, factors, 0)

    plus, minus = ring // 2, ring - 1 - ring // 2
    chains = []
    first = 0
    for half, sign, length in ((0, 1, plus), (0, -1, minus), (1, 1, minus), (1, -1, plus)):
        chains.append((half, sign, length, first))
        first += length
    order = [
        ring // 2 - (k + 1) // 2 if k % 2 == 1 else k // 2 + ring // 2 for k in range(ring)
    ]

    def z_copy(chain, step):
        half, sign, length, first = chain
        return pltpu.make_async_remote_copy(
            src_ref=z_out.at[first + step],
            dst_ref=z_in.at[first + step],
            send_sem=z_send_sem.at[first + step],
            recv_sem=z_recv_sem.at[first + step],
            device_id={"dp": up if sign > 0 else down},
            device_id_type=MESH,
        )

    def own_part(c, half):
        part = acc[c, pl.ds(half * half_blocks, half_blocks)]
        return part.reshape(groups, GROUP, width)

    def z_received(chain, step):
        z_copy(chain, step).wait_recv()
        place = chain[3] + step
        codes = z_in[place, pl.ds(0, values_here)].astype(jnp.int32).astype(jnp.float32)
        scale_code = z_in[place, pl.ds(values_here, CODE_ROWS)].astype(jnp.int32)
        scale = scale_of(scale_code.astype(jnp.float32)[:groups])
        return codes.reshape(groups, GROUP, width) * scale[:, None, :]

    def z_hop(chain, step, c):
        part = own_part(c, chain[0])
        if step:
            part = part + z_received(chain, step - 1)
        codes, scale_code = to_codes(part)
        place = chain[3] + step
        z_out[place, pl.ds(0, values_here)] = codes.reshape(values_here, width)
        if groups < CODE_ROWS:
            scale_code = jnp.concatenate(
                [scale_code, jnp.zeros((CODE_ROWS - groups, width), jnp.float32)], 0
            )
        z_out[place, pl.ds(values_here, CODE_ROWS)] = scale_code.astype(jnp.int32).astype(
            jnp.int16
        )
        z_copy(chain, step).start()

    def query_gradient(slot):
        block = my_block(slot)
        grad_t[...] = jnp.zeros_like(grad_t)

        def candidate(c, _):
            passage = p_turned[block, c]
            for start in range(0, flat, chunk):
                here = pl.ds(start, chunk)
                product = jnp.dot(
                    passage, high[slot, c, :, here], preferred_element_type=jnp.float32
                ) + jnp.dot(passage, low[slot, c, :, here], preferred_element_type=jnp.float32)
                grad_t[:, here] += product * totals[slot, pl.ds(c, 1), here]
            return 0

        lax.fori_loop(0, per_block, candidate, 0)
        pieces = grad_t[...].T.reshape(rows, tokens, width)
        codes, scale_code = to_codes(pieces)
        for tile in range(tiles):
            back_out[:, slot * tiles + tile] = codes[:, tile * CODE_ROWS : (tile + 1) * CODE_ROWS]
        back_scales[slot] = scale_code

    def send_back(offset, _):
        peer = peer_of(offset)
        pltpu.make_async_remote_copy(
            src_ref=back_out.at[peer],
            dst_ref=back_in.at[me],
            send_sem=send_sem.at[2],
            recv_sem=back_sem,
            device_id={"cand": peer},
            device_id_type=MESH,
        ).start()
        return 0

    def start_back():
        filler = jnp.zeros((rows, width), jnp.float32)
        stacked = jnp.stack(
            [back_scales[k] if k < cap else filler for k in range(CODE_ROWS)], 1
        )
        back_out[:, cap * tiles] = stacked.astype(jnp.int32).astype(jnp.int16)
        lax.fori_loop(1, rows, send_back, 0)
        back_in[me] = back_out[me]

    def gradients(step, _):
        near = jnp.where(step % 2 == 1, ring // 2 - (step + 1) // 2, step // 2 + ring // 2)
        c = lax.rem(plane + near, ring)
        acc[c] = jnp.zeros(acc.shape[1:], jnp.float32)

        def one_slot(slot, _):
            block = my_block(slot)
            scaled = q_turned[slot].astype(jnp.float32) * totals[slot, pl.ds(c, 1)]
            scaled_high = scaled.astype(jnp.bfloat16)
            scaled_low = (scaled - scaled_high.astype(jnp.float32)).astype(jnp.bfloat16)
            both = jnp.concatenate([scaled_high, scaled_low], 0)
            along = (((1,), (1,)), ((), ()))
            first = lax.dot_general(
                high[slot, c], both, along, preferred_element_type=jnp.float32
            )
            passage_grad = (
                first[:, :width]
                + first[:, width:]
                + lax.dot_general(
                    low[slot, c], scaled_high, along, preferred_element_type=jnp.float32
                )
            )
            for local in range(blocks_here):
                chosen = jnp.where(block == local, 1.0, 0.0)
                acc[c, local] += chosen * passage_grad
            return 0

        lax.fori_loop(0, cap, one_slot, 0)
        for k in range(per_block):

            @pl.when(step == k)
            def _(k=k):
                for chain in chains:
                    half, sign, length, first = chain
                    for hop in range(length):
                        if (sign * (length - hop) - order[k]) % ring == 0:
                            z_hop(chain, hop, c)

        @pl.when(step < cap)
        def _():
            query_gradient(step)

        @pl.when(step == cap - 1)
        def _():
            start_back()

        return 0

    lax.fori_loop(0, per_block, gradients, 0)

    def loss_row(block_row, _):
        first = scores_of(place_of(2 * block_row))
        second = scores_of(place_of(2 * block_row + 1))
        log_total = jnp.log(
            jnp.sum(jnp.exp(first), 0, keepdims=True) + jnp.sum(jnp.exp(second), 0, keepdims=True)
        )
        positive = positives(block_row)
        chosen = jnp.sum(jnp.where(column == positive, first, 0.0), 0, keepdims=True) + jnp.sum(
            jnp.where(column + per_block == positive, second, 0.0), 0, keepdims=True
        )
        here = lax.broadcasted_iota(jnp.int32, (1, rows), 1) == me
        loss = jnp.sum(jnp.where(here, log_total - chosen, 0.0), 1, keepdims=True)
        loss_ref[pl.ds(block_row, 1)] = loss
        return 0

    lax.fori_loop(0, row_blocks, loss_row, 0)

    for half in range(2):
        result = own_part(plane, half)
        for chain in chains:
            if chain[0] == half and chain[2]:
                result = result + z_received(chain, chain[2] - 1)
        passage_out[pl.ds(half * half_blocks, half_blocks)] = result.reshape(
            half_blocks, passage_len, width
        )

    pltpu.make_async_copy(back_in.at[others], back_in.at[others], back_sem).wait()
    scale_row = lax.broadcasted_iota(jnp.int32, (CODE_ROWS, width), 0)

    def piece(place):
        owner, slot = place // cap, place % cap
        codes = [back_in[owner, slot * tiles + tile] for tile in range(tiles)]
        codes = jnp.concatenate([c.astype(jnp.int32) for c in codes], 0).astype(jnp.float32)
        scale_code = back_in[owner, cap * tiles].astype(jnp.int32)
        scale_code = jnp.sum(jnp.where(scale_row == slot, scale_code, 0), 0, keepdims=True)
        return codes * scale_of(scale_code.astype(jnp.float32))

    def add_pair(block_row, _):
        query_out[block_row] = piece(place_of(2 * block_row)) + piece(place_of(2 * block_row + 1))
        return 0

    lax.fori_loop(0, row_blocks, add_pair, 0)

    for slot in range(cap):
        pltpu.make_async_copy(q_slot.at[slot, head], q_slot.at[slot, head], send_sem.at[0]).wait()
    pltpu.make_async_copy(scores.at[others], scores.at[others], send_sem.at[1]).wait()
    pltpu.make_async_copy(back_in.at[others], back_in.at[others], send_sem.at[2]).wait()
    for chain in chains:
        for step in range(chain[2]):
            z_copy(chain, step).wait_send()


def finish_kernel(*refs):
    for source, target in zip(refs[:3], refs[3:]):
        target[...] = source[...]


def on_device(rows, ring, queries, passages, cand_ids, pos_index):
    row_blocks, _, tokens, width = queries.shape
    blocks_here, per_block, passage_len, _ = passages.shape
    requests = 2 * row_blocks
    cap = 4 * ((requests + rows - 1) // rows)
    flat = rows * tokens
    smem = pl.BlockSpec(memory_space=pltpu.SMEM)
    vmem = pl.BlockSpec(memory_space=pltpu.VMEM)
    half_blocks = blocks_here // 2
    hops = 2 * (ring - 1)
    f32, bf16, i16 = jnp.float32, jnp.bfloat16, jnp.int16
    out_shape = (
        jax.ShapeDtypeStruct((row_blocks, 1), f32),
        jax.ShapeDtypeStruct((row_blocks, tokens, width), f32),
        jax.ShapeDtypeStruct((blocks_here, passage_len, width), f32),
    )
    z_rows = half_blocks * passage_len + CODE_ROWS
    back_tiles = cap * tokens // CODE_ROWS + 1
    results = pl.pallas_call(
        functools.partial(main_kernel, rows, ring, cap),
        out_shape=out_shape,
        in_specs=[smem] + [vmem] * 3,
        out_specs=(vmem, vmem, vmem),
        scratch_shapes=[
            pltpu.VMEM((8, LANES), jnp.int32),
            pltpu.SMEM((8, LANES), jnp.int32),
            pltpu.VMEM((cap, rows, tokens, width), bf16),
            pltpu.VMEM((cap, flat, width), bf16),
            pltpu.VMEM((cap, width, flat), bf16),
            pltpu.VMEM((blocks_here, per_block, width, passage_len), bf16),
            pltpu.VMEM((cap, per_block, passage_len, flat), bf16),
            pltpu.VMEM((cap, per_block, passage_len, flat), bf16),
            pltpu.VMEM((cap, per_block, flat), f32),
            pltpu.VMEM((rows, per_block, LANES), f32),
            pltpu.VMEM((width, flat), f32),
            pltpu.VMEM((cap, rows, width), f32),
            pltpu.VMEM((rows, back_tiles, CODE_ROWS, width), i16),
            pltpu.VMEM((rows, back_tiles, CODE_ROWS, width), i16),
            pltpu.VMEM((per_block, blocks_here, passage_len, width), f32),
            pltpu.VMEM((hops, z_rows, width), i16),
            pltpu.VMEM((hops, z_rows, width), i16),
            pltpu.SemaphoreType.DMA,
            pltpu.SemaphoreType.DMA((3,)),
            pltpu.SemaphoreType.DMA((cap,)),
            pltpu.SemaphoreType.DMA,
            pltpu.SemaphoreType.DMA,
            pltpu.SemaphoreType.DMA((hops,)),
            pltpu.SemaphoreType.DMA((hops,)),
        ],
        compiler_params=pltpu.CompilerParams(
            collective_id=0, has_side_effects=True, vmem_limit_bytes=60 * 1024 * 1024
        ),
        name="late_interaction",
    )(
        cand_ids,
        queries.reshape(row_blocks, tokens, width),
        passages,
        pos_index,
    )
    losses, query_grads, passage_grads = pl.pallas_call(
        finish_kernel,
        out_shape=out_shape,
        in_specs=[vmem] * 3,
        out_specs=(vmem, vmem, vmem),
        name="results",
    )(*results)
    return (losses, query_grads[:, None], passage_grads[:, None])


def solution(mesh):
    in_specs = (
        P("dp", "cand", None, None),
        P("cand", None, None, None),
        P("dp", None),
        P("dp", None),
    )
    out_specs = (P("dp", "cand"), P("dp", "cand", None, None), P("cand", "dp", None, None))
    return jax.shard_map(
        functools.partial(on_device, mesh.shape["cand"], mesh.shape["dp"]),
        mesh=mesh,
        in_specs=in_specs,
        out_specs=out_specs,
        check_vma=False,
    )
```

time: 100 us -> 85.7 us (0.86)
  Pallas kernels: 93.2 us -> 82.2 us
  local copies, waits for them, and re-layouts: 6.18 us -> 2.63 us
    pallas_call x1, Pallas kernels: 90.4 us -> 80.2 us  [on_device(): pl.pallas_call(functools.partial(main_kernel, rows, ring, cap), out_shape...]
    unnamed x4 -> x2, local copies, waits for them, and re-layouts: 5.58 us -> 2.63 us
where the time goes in v2:
time: 85.7 us; the launch traced here: 85.5 us
  Pallas kernels  82.2 us (96%)
  local copies, waits for them, and re-layouts  2.63 us (3%)
    pallas_call x1, Pallas kernels, on_device(): pl.pallas_call(functools.partial(main_kernel, rows, ring, cap), out_shape...  80.2 us
    unnamed x2, local copies, waits for them, and re-layouts  2.63 us
    pallas_call x1, Pallas kernels, on_device(): pl.pallas_call(finish_kernel, out_shape=out_shape, in_specs=[vmem] * 3, o...  2.04 us

profile of v2, /device:TPU:1, one launch (start us, length us, event | category | flops | bytes accessed | tf_op | source)
XLA Modules:
  0.0 85.5 jit_solution(7542454417060411285)
XLA Ops:
  0.6 1.4 %copy.7.ids_ref = s32[16,2]{1,0:T(8,128)} copy(s32[16,2]{0,1:T(2,128)} %param.6) | data formatting | bytes 256 | tf_op args[2]
  2.0 80.2 %late_interaction.1 = (f32[16,1]{1,0:T(8,128)}, f32[16,32,128]{2,1,0:T(8,128)}, f32[4,256,128]{2,1,0:T(8,128)}) custom-call(s32[16,2]{1,0:T(8,128)} %copy.7.ids_ref, bf16[16,32,128]{2,1,0:T(8,128)(2,1)} %bitcast.7, bf16[4,8,256,128]{3,2,1,0:T(8,128)(2,1)} %p_ref.1, s32[16,32]{1,0:T(8,128)} %pos_ref.1), custom_call_target="tpu_custom_call" | custom-call | tf_op jit(solution)/shard_map/late_interaction/pallas_call | solution.py:480
  82.2 2.0 %results.1 = (f32[16,1]{1,0:T(8,128)}, f32[16,32,128]{2,1,0:T(8,128)}, f32[4,256,128]{2,1,0:T(8,128)}) custom-call(f32[16,1]{1,0:T(8,128)} %get-tuple-element.9.refs_0_, f32[16,32,128]{2,1,0:T(8,128)} %get-tuple-element.10.refs_1_, f32[4,256,128]{2,1,0:T(8,128)} %get-tuple-element.11.refs_2_), custom_call_target="tpu_custom_call" | custom-call | tf_op jit(solution)/shard_map/results/pallas_call | solution.py:521
  84.2 1.3 %copy.8 = f32[16,1]{0,1:T(1,128)} copy(f32[16,1]{1,0:T(8,128)} %get-tuple-element.15) | data formatting | bytes 128

commit v3 on v2

--- a/solution.py
+++ b/solution.py
@@ -36,23 +36,23 @@
 
 def fill_tables(blocks_here, cap, ids_ref, table):
     count = ids_ref.shape[0] * ids_ref.shape[1]
-    columns = ids_ref.shape[1]
     along = lax.broadcasted_iota(jnp.int32, (count, LANES), 1)
     down = lax.broadcasted_iota(jnp.int32, (count, LANES), 0)
-    owner_along = jnp.full((count, LANES), -1, jnp.int32)
-    owner_down = jnp.full((count, LANES), -1, jnp.int32)
-    for request in range(count):
-        owner = ids_ref[request // columns, request % columns] // blocks_here
-        owner_along = jnp.where(along == request, owner, owner_along)
-        owner_down = jnp.where(down == request, owner, owner_down)
-    same = owner_along == owner_down
+    ids = jnp.concatenate([ids_ref[:, :1], ids_ref[:, 1:]], 0)
+    ids_down = jnp.broadcast_to(ids, (count, LANES))
+    owner_down = ids_down // blocks_here
+    owner_along = jnp.sum(jnp.where(along == down, owner_down, 0), 0, keepdims=True)
+    same = (owner_along == owner_down) & (along < count)
     rank_along = jnp.sum((same & (down < along)).astype(jnp.int32), 0, keepdims=True)
-    place_along = owner_along[:1] * cap + rank_along
+    place_along = owner_along * cap + rank_along
     rank_down = jnp.sum((same & (along < down)).astype(jnp.int32), 1, keepdims=True)
     here = owner_down * cap + rank_down == along
     request_along = jnp.sum(jnp.where(here, down + 1, 0), 0, keepdims=True) - 1
+    block_along = jnp.sum(jnp.where(here, ids_down % blocks_here, 0), 0, keepdims=True)
     row = lax.broadcasted_iota(jnp.int32, table.shape, 0)
-    table[...] = jnp.where(row == 0, request_along, place_along)
+    table[...] = jnp.where(
+        row == 0, request_along, jnp.where(row == 1, place_along, block_along)
+    )
 
 
 def main_kernel(
@@ -76,6 +76,9 @@
     low,
     totals,
     scores,
+    products,
+    scaled_even,
+    scaled_odd,
     grad_t,
     back_scales,
     back_out,
@@ -101,6 +104,7 @@
     groups = half_blocks * passage_len // GROUP
     values_here = half_blocks * passage_len
     tiles = tokens // CODE_ROWS
+    group_slots = cap // 2
 
     def peer_of(offset):
         return lax.rem(me + offset, rows)
@@ -132,7 +136,7 @@
     def fill(owner, _):
         for slot in range(cap):
             request = jnp.maximum(request_at(owner * cap + slot), 0)
-            q_send[slot, owner] = q_ref[request // 2]
+            q_send[slot, owner] = q_ref[request % row_blocks]
         return 0
 
     lax.fori_loop(0, rows, fill, 0)
@@ -174,15 +178,14 @@
         return request_at(me * cap + slot)
 
     def my_block(slot):
-        request = jnp.maximum(my_request(slot), 0)
-        return ids_ref[request // 2, request % 2] % blocks_here
+        return table_s[2, me * cap + slot]
 
     def forward(slot, my_scores):
         pltpu.make_async_copy(q_slot.at[slot, head], q_slot.at[slot, head], q_sem.at[slot]).wait()
         block = my_block(slot)
         q_turned[slot] = q_slot[slot].T
 
-        def candidate(c, _):
+        for c in range(per_block):
             passage = p_ref[block, c]
             for start in range(0, flat, chunk):
                 here = pl.ds(start, chunk)
@@ -195,10 +198,7 @@
                 low[slot, c, :, here] = (exponent - rounded.astype(jnp.float32)).astype(
                     jnp.bfloat16
                 )
-                totals[slot, pl.ds(c, 1), here] = jnp.sum(exponent, 0, keepdims=True)
-            return 0
-
-        lax.fori_loop(0, per_block, candidate, 0)
+                totals[slot, c : c + 1, here] = jnp.sum(exponent, 0, keepdims=True)
         soft_max = softness * jnp.log(totals[slot])
         place = (query_of + slot * rows == lane).astype(jnp.float32)
         return my_scores + jnp.dot(
@@ -220,6 +220,23 @@
         return 0
 
     lax.fori_loop(1, rows, send_scores, 0)
+    early = products.shape[0]
+
+    def product(slot, block, c, here):
+        passage = p_turned[block, c]
+        return jnp.dot(
+            passage, high[slot, c, :, here], preferred_element_type=jnp.float32
+        ) + jnp.dot(passage, low[slot, c, :, here], preferred_element_type=jnp.float32)
+
+    def early_products(slot, _):
+        block = my_block(slot)
+        for c in range(per_block):
+            for start in range(0, flat, chunk):
+                here = pl.ds(start, chunk)
+                products[slot, c, :, here] = product(slot, block, c, here)
+        return 0
+
+    lax.fori_loop(0, early, early_products, 0)
     others = pl.ds(0, rows - 1)
     pltpu.make_async_copy(scores.at[others], scores.at[others], score_sem).wait()
 
@@ -247,9 +264,9 @@
         request = my_request(slot)
         valid = jnp.where(request >= 0, loss_scale, 0.0)
         request = jnp.maximum(request, 0)
-        block_row, half = request // 2, request % 2
+        block_row, half = request % row_blocks, request // row_blocks
         mine = scores_of(me * cap + slot)
-        other = scores_of(place_of(block_row * 2 + 1 - half))
+        other = scores_of(place_of((1 - half) * row_blocks + block_row))
         log_total = jnp.log(
             jnp.sum(jnp.exp(mine), 0, keepdims=True) + jnp.sum(jnp.exp(other), 0, keepdims=True)
         )
@@ -282,8 +299,8 @@
             device_id_type=MESH,
         )
 
-    def own_part(c, half):
-        part = acc[c, pl.ds(half * half_blocks, half_blocks)]
+    def own_part(half):
+        part = acc[pl.ds(half * half_blocks, half_blocks)]
         return part.reshape(groups, GROUP, width)
 
     def z_received(chain, step):
@@ -294,8 +311,8 @@
         scale = scale_of(scale_code.astype(jnp.float32)[:groups])
         return codes.reshape(groups, GROUP, width) * scale[:, None, :]
 
-    def z_hop(chain, step, c):
-        part = own_part(c, chain[0])
+    def z_hop(chain, step):
+        part = own_part(chain[0])
         if step:
             part = part + z_received(chain, step - 1)
         codes, scale_code = to_codes(part)
@@ -310,76 +327,98 @@
         )
         z_copy(chain, step).start()
 
-    def query_gradient(slot):
+    def code_pieces(slot):
+        codes, scale_code = to_codes(grad_t[...].T.reshape(rows, tokens, width))
+        group, inner = slot // group_slots, slot % group_slots
+        for tile in range(tiles):
+            back_out[group, :, inner * tiles + tile] = codes[
+                :, tile * CODE_ROWS : (tile + 1) * CODE_ROWS
+            ]
+        back_scales[slot] = scale_code
+
+    def early_gradient(slot, _):
+        for start in range(0, flat, chunk):
+            here = pl.ds(start, chunk)
+            grad_t[:, here] = sum(
+                products[slot, c, :, here] * totals[slot, c : c + 1, here]
+                for c in range(per_block)
+            )
+        code_pieces(slot)
+        return 0
+
+    def late_gradient(slot, _):
         block = my_block(slot)
-        grad_t[...] = jnp.zeros_like(grad_t)
-
-        def candidate(c, _):
-            passage = p_turned[block, c]
-            for start in range(0, flat, chunk):
-                here = pl.ds(start, chunk)
-                product = jnp.dot(
-                    passage, high[slot, c, :, here], preferred_element_type=jnp.float32
-                ) + jnp.dot(passage, low[slot, c, :, here], preferred_element_type=jnp.float32)
-                grad_t[:, here] += product * totals[slot, pl.ds(c, 1), here]
-            return 0
-
-        lax.fori_loop(0, per_block, candidate, 0)
-        pieces = grad_t[...].T.reshape(rows, tokens, width)
-        codes, scale_code = to_codes(pieces)
-        for tile in range(tiles):
-            back_out[:, slot * tiles + tile] = codes[:, tile * CODE_ROWS : (tile + 1) * CODE_ROWS]
-        back_scales[slot] = scale_code
-
-    def send_back(offset, _):
-        peer = peer_of(offset)
-        pltpu.make_async_remote_copy(
-            src_ref=back_out.at[peer],
-            dst_ref=back_in.at[me],
-            send_sem=send_sem.at[2],
-            recv_sem=back_sem,
-            device_id={"cand": peer},
-            device_id_type=MESH,
-        ).start()
-        return 0
-
-    def start_back():
+        for start in range(0, flat, chunk):
+            here = pl.ds(start, chunk)
+            grad_t[:, here] = sum(
+                product(slot, block, c, here) * totals[slot, c : c + 1, here]
+                for c in range(per_block)
+            )
+        code_pieces(slot)
+        return 0
+
+    def start_back(group):
         filler = jnp.zeros((rows, width), jnp.float32)
         stacked = jnp.stack(
-            [back_scales[k] if k < cap else filler for k in range(CODE_ROWS)], 1
-        )
-        back_out[:, cap * tiles] = stacked.astype(jnp.int32).astype(jnp.int16)
+            [
+                back_scales[group * group_slots + k] if k < group_slots else filler
+                for k in range(CODE_ROWS)
+            ],
+            1,
+        )
+        back_out[group, :, group_slots * tiles] = stacked.astype(jnp.int32).astype(jnp.int16)
+
+        def send_back(offset, _):
+            peer = peer_of(offset)
+            pltpu.make_async_remote_copy(
+                src_ref=back_out.at[group, peer],
+                dst_ref=back_in.at[group, me],
+                send_sem=send_sem.at[2 + group],
+                recv_sem=back_sem.at[group],
+                device_id={"cand": peer},
+                device_id_type=MESH,
+            ).start()
+            return 0
+
         lax.fori_loop(1, rows, send_back, 0)
-        back_in[me] = back_out[me]
+        back_in[group, me] = back_out[group, me]
+
+    def passage_at(step):
+        near = jnp.where(step % 2 == 1, ring // 2 - (step + 1) // 2, step // 2 + ring // 2)
+        return lax.rem(plane + near, ring)
+
+    def prepare(buffer, slot, c):
+        value = q_turned[slot].astype(jnp.float32) * totals[slot, pl.ds(c, 1)]
+        value_high = value.astype(jnp.bfloat16)
+        buffer[:width] = value_high
+        buffer[width:] = (value - value_high.astype(jnp.float32)).astype(jnp.bfloat16)
+
+    prepare(scaled_even, 0, passage_at(0))
 
     def gradients(step, _):
-        near = jnp.where(step % 2 == 1, ring // 2 - (step + 1) // 2, step // 2 + ring // 2)
-        c = lax.rem(plane + near, ring)
-        acc[c] = jnp.zeros(acc.shape[1:], jnp.float32)
-
-        def one_slot(slot, _):
-            block = my_block(slot)
-            scaled = q_turned[slot].astype(jnp.float32) * totals[slot, pl.ds(c, 1)]
-            scaled_high = scaled.astype(jnp.bfloat16)
-            scaled_low = (scaled - scaled_high.astype(jnp.float32)).astype(jnp.bfloat16)
-            both = jnp.concatenate([scaled_high, scaled_low], 0)
+        c = passage_at(step)
+        sums = [0.0] * blocks_here
+        for slot in range(cap):
+            now, later = (
+                (scaled_even, scaled_odd) if slot % 2 == 0 else (scaled_odd, scaled_even)
+            )
+            if slot < cap - 1:
+                prepare(later, slot + 1, c)
+            else:
+                prepare(later, 0, passage_at(lax.rem(step + 1, per_block)))
             along = (((1,), (1,)), ((), ()))
             first = lax.dot_general(
-                high[slot, c], both, along, preferred_element_type=jnp.float32
+                high[slot, c], now[...], along, preferred_element_type=jnp.float32
             )
-            passage_grad = (
-                first[:, :width]
-                + first[:, width:]
-                + lax.dot_general(
-                    low[slot, c], scaled_high, along, preferred_element_type=jnp.float32
-                )
+            second = lax.dot_general(
+                low[slot, c], now[:width], along, preferred_element_type=jnp.float32
             )
+            passage_grad = first[:, :width] + first[:, width:] + second
             for local in range(blocks_here):
-                chosen = jnp.where(block == local, 1.0, 0.0)
-                acc[c, local] += chosen * passage_grad
-            return 0
-
-        lax.fori_loop(0, cap, one_slot, 0)
+                chosen = jnp.where(my_block(slot) == local, 1.0, 0.0)
+                sums[local] = sums[local] + chosen * passage_grad
+        for local in range(blocks_here):
+            acc[local] = sums[local]
         for k in range(per_block):
 
             @pl.when(step == k)
@@ -388,23 +427,28 @@
                     half, sign, length, first = chain
                     for hop in range(length):
                         if (sign * (length - hop) - order[k]) % ring == 0:
-                            z_hop(chain, hop, c)
-
-        @pl.when(step < cap)
+                            z_hop(chain, hop)
+
+        @pl.when(step == 0)
         def _():
-            query_gradient(step)
-
-        @pl.when(step == cap - 1)
+            lax.fori_loop(0, early, early_gradient, 0)
+            start_back(0)
+
+        @pl.when((step > 0) & (step <= cap - early))
         def _():
-            start_back()
+            late_gradient(early + step - 1, 0)
+
+        @pl.when(step == cap - early)
+        def _():
+            start_back(1)
 
         return 0
 
     lax.fori_loop(0, per_block, gradients, 0)
 
-    def loss_row(block_row, _):
-        first = scores_of(place_of(2 * block_row))
-        second = scores_of(place_of(2 * block_row + 1))
+    def loss_row(block_row, losses):
+        first = scores_of(place_of(block_row))
+        second = scores_of(place_of(row_blocks + block_row))
         log_total = jnp.log(
             jnp.sum(jnp.exp(first), 0, keepdims=True) + jnp.sum(jnp.exp(second), 0, keepdims=True)
         )
@@ -414,13 +458,15 @@
         )
         here = lax.broadcasted_iota(jnp.int32, (1, rows), 1) == me
         loss = jnp.sum(jnp.where(here, log_total - chosen, 0.0), 1, keepdims=True)
-        loss_ref[pl.ds(block_row, 1)] = loss
-        return 0
-
-    lax.fori_loop(0, row_blocks, loss_row, 0)
+        return jnp.where(loss_lane == block_row, loss, losses)
+
+    loss_lane = lax.broadcasted_iota(jnp.int32, (1, row_blocks), 1)
+    loss_ref[...] = lax.fori_loop(
+        0, row_blocks, loss_row, jnp.zeros((1, row_blocks), jnp.float32)
+    )
 
     for half in range(2):
-        result = own_part(plane, half)
+        result = own_part(half)
         for chain in chains:
             if chain[0] == half and chain[2]:
                 result = result + z_received(chain, chain[2] - 1)
@@ -428,19 +474,23 @@
             half_blocks, passage_len, width
         )
 
-    pltpu.make_async_copy(back_in.at[others], back_in.at[others], back_sem).wait()
+    for group in range(2):
+        back_others = back_in.at[group, others]
+        pltpu.make_async_copy(back_others, back_others, back_sem.at[group]).wait()
     scale_row = lax.broadcasted_iota(jnp.int32, (CODE_ROWS, width), 0)
 
     def piece(place):
         owner, slot = place // cap, place % cap
-        codes = [back_in[owner, slot * tiles + tile] for tile in range(tiles)]
+        group, inner = slot // group_slots, slot % group_slots
+        codes = [back_in[group, owner, inner * tiles + tile] for tile in range(tiles)]
         codes = jnp.concatenate([c.astype(jnp.int32) for c in codes], 0).astype(jnp.float32)
-        scale_code = back_in[owner, cap * tiles].astype(jnp.int32)
-        scale_code = jnp.sum(jnp.where(scale_row == slot, scale_code, 0), 0, keepdims=True)
+        scale_code = back_in[group, owner, group_slots * tiles].astype(jnp.int32)
+        scale_code = jnp.sum(jnp.where(scale_row == inner, scale_code, 0), 0, keepdims=True)
         return codes * scale_of(scale_code.astype(jnp.float32))
 
     def add_pair(block_row, _):
-        query_out[block_row] = piece(place_of(2 * block_row)) + piece(place_of(2 * block_row + 1))
+        second = place_of(row_blocks + block_row)
+        query_out[block_row] = piece(place_of(block_row)) + piece(second)
         return 0
 
     lax.fori_loop(0, row_blocks, add_pair, 0)
@@ -448,7 +498,9 @@
     for slot in range(cap):
         pltpu.make_async_copy(q_slot.at[slot, head], q_slot.at[slot, head], send_sem.at[0]).wait()
     pltpu.make_async_copy(scores.at[others], scores.at[others], send_sem.at[1]).wait()
-    pltpu.make_async_copy(back_in.at[others], back_in.at[others], send_sem.at[2]).wait()
+    for group in range(2):
+        back_others = back_in.at[group, others]
+        pltpu.make_async_copy(back_others, back_others, send_sem.at[2 + group]).wait()
     for chain in chains:
         for step in range(chain[2]):
             z_copy(chain, step).wait_send()
@@ -465,22 +517,21 @@
     requests = 2 * row_blocks
     cap = 4 * ((requests + rows - 1) // rows)
     flat = rows * tokens
-    smem = pl.BlockSpec(memory_space=pltpu.SMEM)
     vmem = pl.BlockSpec(memory_space=pltpu.VMEM)
     half_blocks = blocks_here // 2
     hops = 2 * (ring - 1)
     f32, bf16, i16 = jnp.float32, jnp.bfloat16, jnp.int16
     out_shape = (
-        jax.ShapeDtypeStruct((row_blocks, 1), f32),
+        jax.ShapeDtypeStruct((1, row_blocks), f32),
         jax.ShapeDtypeStruct((row_blocks, tokens, width), f32),
         jax.ShapeDtypeStruct((blocks_here, passage_len, width), f32),
     )
     z_rows = half_blocks * passage_len + CODE_ROWS
-    back_tiles = cap * tokens // CODE_ROWS + 1
+    back_tiles = cap // 2 * tokens // CODE_ROWS + 1
     results = pl.pallas_call(
         functools.partial(main_kernel, rows, ring, cap),
         out_shape=out_shape,
-        in_specs=[smem] + [vmem] * 3,
+        in_specs=[vmem] * 4,
         out_specs=(vmem, vmem, vmem),
         scratch_shapes=[
             pltpu.VMEM((8, LANES), jnp.int32),
@@ -493,23 +544,26 @@
             pltpu.VMEM((cap, per_block, passage_len, flat), bf16),
             pltpu.VMEM((cap, per_block, flat), f32),
             pltpu.VMEM((rows, per_block, LANES), f32),
+            pltpu.VMEM((cap // 2, per_block, width, flat), f32),
+            pltpu.VMEM((2 * width, flat), bf16),
+            pltpu.VMEM((2 * width, flat), bf16),
             pltpu.VMEM((width, flat), f32),
             pltpu.VMEM((cap, rows, width), f32),
-            pltpu.VMEM((rows, back_tiles, CODE_ROWS, width), i16),
-            pltpu.VMEM((rows, back_tiles, CODE_ROWS, width), i16),
-            pltpu.VMEM((per_block, blocks_here, passage_len, width), f32),
+            pltpu.VMEM((2, rows, back_tiles, CODE_ROWS, width), i16),
+            pltpu.VMEM((2, rows, back_tiles, CODE_ROWS, width), i16),
+            pltpu.VMEM((blocks_here, passage_len, width), f32),
             pltpu.VMEM((hops, z_rows, width), i16),
             pltpu.VMEM((hops, z_rows, width), i16),
             pltpu.SemaphoreType.DMA,
-            pltpu.SemaphoreType.DMA((3,)),
+            pltpu.SemaphoreType.DMA((4,)),
             pltpu.SemaphoreType.DMA((cap,)),
             pltpu.SemaphoreType.DMA,
-            pltpu.SemaphoreType.DMA,
+            pltpu.SemaphoreType.DMA((2,)),
             pltpu.SemaphoreType.DMA((hops,)),
             pltpu.SemaphoreType.DMA((hops,)),
         ],
         compiler_params=pltpu.CompilerParams(
-            collective_id=0, has_side_effects=True, vmem_limit_bytes=60 * 1024 * 1024
+            collective_id=0, has_side_effects=True, vmem_limit_bytes=62 * 1024 * 1024
         ),
         name="late_interaction",
     )(
@@ -525,7 +579,7 @@
         out_specs=(vmem, vmem, vmem),
         name="results",
     )(*results)
-    return (losses, query_grads[:, None], passage_grads[:, None])
+    return (losses.reshape(row_blocks, 1), query_grads[:, None], passage_grads[:, None])
 
 
 def solution(mesh):

time: 85.7 us -> 72.8 us (0.85)
  Pallas kernels: 82.2 us -> 70.5 us
  local copies, waits for them, and re-layouts: 2.63 us -> 1.35 us
    pallas_call x1, Pallas kernels: 80.2 us -> 68.5 us  [on_device(): pl.pallas_call(functools.partial(main_kernel, rows, ring, cap), out_shape...]
    unnamed x2 -> x1, local copies, waits for them, and re-layouts: 2.63 us -> 1.35 us
where the time goes in v3:
time: 72.8 us; the launch traced here: 72.5 us
  Pallas kernels  70.5 us (97%)
  local copies, waits for them, and re-layouts  1.35 us (2%)
    pallas_call x1, Pallas kernels, on_device(): pl.pallas_call(functools.partial(main_kernel, rows, ring, cap), out_shape...  68.5 us
    pallas_call x1, Pallas kernels, on_device(): pl.pallas_call(finish_kernel, out_shape=out_shape, in_specs=[vmem] * 3, o...  2.03 us

profile of v3, /device:TPU:1, one launch (start us, length us, event | category | flops | bytes accessed | tf_op | source)
XLA Modules:
  0.0 72.5 jit_solution(13267018044582584692)
XLA Ops:
  0.6 1.4 %copy.7.ids_ref = s32[16,2]{1,0:T(8,128)} copy(s32[16,2]{0,1:T(2,128)} %param.6) | data formatting | bytes 256 | tf_op args[2]
  2.0 68.5 %late_interaction.1 = (f32[1,16]{1,0:T(1,128)}, f32[16,32,128]{2,1,0:T(8,128)}, f32[4,256,128]{2,1,0:T(8,128)}) custom-call(s32[16,2]{1,0:T(8,128)} %copy.7.ids_ref, bf16[16,32,128]{2,1,0:T(8,128)(2,1)} %bitcast.8, bf16[4,8,256,128]{3,2,1,0:T(8,128)(2,1)} %p_ref.1, s32[16,32]{1,0:T(8,128)} %pos_ref.1), custom_call_target="tpu_custom_call" | custom-call | tf_op jit(solution)/shard_map/late_interaction/pallas_call | solution.py:531
  70.4 2.0 %results.1 = (f32[1,16]{1,0:T(1,128)}, f32[16,32,128]{2,1,0:T(8,128)}, f32[4,256,128]{2,1,0:T(8,128)}) custom-call(f32[1,16]{1,0:T(1,128)} %get-tuple-element.9.refs_0_, f32[16,32,128]{2,1,0:T(8,128)} %get-tuple-element.10.refs_1_, f32[4,256,128]{2,1,0:T(8,128)} %get-tuple-element.11.refs_2_), custom_call_target="tpu_custom_call" | custom-call | tf_op jit(solution)/shard_map/results/pallas_call | solution.py:575

commit v4 on v3

--- a/solution.py
+++ b/solution.py
@@ -20,6 +20,26 @@
 TINY = 1e-30
 GROUP = 32
 CHUNK = 256
+Q_GROUP = 1
+ACC_SLOTS = 4
+SCHEDULES = {
+    8: (
+        ("A+0", "B-0", "e0"),
+        ("B+0", "e1", "k0"),
+        ("A-0", "A+1", "B-1"),
+        ("l2",),
+        ("B+1", "A-1"),
+        ("l3", "k1", "A+2", "B-2"),
+        ("B+2", "A-2", "A+3", "B-3"),
+        (),
+    ),
+    4: (
+        ("A+0", "B-0"),
+        ("B+0", "e0", "e1", "k0"),
+        ("A-0", "A+1", "B-1", "l2"),
+        ("l3", "k1"),
+    ),
+}
 
 
 def to_codes(values):
@@ -38,8 +58,14 @@
     count = ids_ref.shape[0] * ids_ref.shape[1]
     along = lax.broadcasted_iota(jnp.int32, (count, LANES), 1)
     down = lax.broadcasted_iota(jnp.int32, (count, LANES), 0)
-    ids = jnp.concatenate([ids_ref[:, :1], ids_ref[:, 1:]], 0)
-    ids_down = jnp.broadcast_to(ids, (count, LANES))
+    row_blocks = ids_ref.shape[1]
+    halves = [jnp.broadcast_to(ids_ref[h : h + 1], (row_blocks, row_blocks)) for h in range(2)]
+    square = (row_blocks, row_blocks)
+    diagonal = lax.broadcasted_iota(jnp.int32, square, 0) == lax.broadcasted_iota(
+        jnp.int32, square, 1
+    )
+    columns = [jnp.sum(jnp.where(diagonal, half, 0), 1, keepdims=True) for half in halves]
+    ids_down = jnp.broadcast_to(jnp.concatenate(columns, 0), (count, LANES))
     owner_down = ids_down // blocks_here
     owner_along = jnp.sum(jnp.where(along == down, owner_down, 0), 0, keepdims=True)
     same = (owner_along == owner_down) & (along < count)
@@ -100,11 +126,12 @@
     chunk = min(CHUNK, flat)
     me = lax.axis_index("cand")
     plane = lax.axis_index("dp")
-    half_blocks = blocks_here // 2
-    groups = half_blocks * passage_len // GROUP
-    values_here = half_blocks * passage_len
+    groups = passage_len // GROUP
     tiles = tokens // CODE_ROWS
     group_slots = cap // 2
+
+    head = pl.ds(0, flat - tokens)
+    q_group = q_send.shape[2]
 
     def peer_of(offset):
         return lax.rem(me + offset, rows)
@@ -136,31 +163,38 @@
     def fill(owner, _):
         for slot in range(cap):
             request = jnp.maximum(request_at(owner * cap + slot), 0)
-            q_send[slot, owner] = q_ref[request % row_blocks]
+            q_send[slot // q_group, owner, slot % q_group] = q_ref[request % row_blocks]
         return 0
 
     lax.fori_loop(0, rows, fill, 0)
     my_rows = pl.ds(pl.multiple_of(me * tokens, tokens), tokens)
     pl.semaphore_wait(barrier, rows - 1 + 2)
 
-    def q_copy(slot, peer):
-        return pltpu.make_async_remote_copy(
-            src_ref=q_send.at[slot, peer],
-            dst_ref=q_slot.at[slot, my_rows],
-            send_sem=send_sem.at[0],
-            recv_sem=q_sem.at[slot],
-            device_id={"cand": peer},
-            device_id_type=MESH,
-        )
-
+    def send_group(group):
+        slots = pl.ds(group * q_group, q_group)
+
+        def send_queries(offset, _):
+            peer = peer_of(offset)
+            pltpu.make_async_remote_copy(
+                src_ref=q_send.at[group, peer],
+                dst_ref=q_slot.at[slots, my_rows],
+                send_sem=send_sem.at[0],
+                recv_sem=q_sem.at[group],
+                device_id={"cand": peer},
+                device_id_type=MESH,
+            ).start()
+            return 0
+
+        lax.fori_loop(1, rows, send_queries, 0)
+
+    def q_wait(group, sem):
+        arrived = q_slot.at[pl.ds(group * q_group, q_group), head]
+        pltpu.make_async_copy(arrived, arrived, sem).wait()
+
+    for group in range(cap // q_group):
+        send_group(group)
     for slot in range(cap):
-
-        def send_queries(offset, _, slot=slot):
-            q_copy(slot, peer_of(offset)).start()
-            return 0
-
-        lax.fori_loop(1, rows, send_queries, 0)
-        q_slot[slot, my_rows] = q_send[slot, me]
+        q_slot[slot, my_rows] = q_send[slot // q_group, me, slot % q_group]
 
     def turn_passage(c, _):
         for block in range(blocks_here):
@@ -169,7 +203,6 @@
 
     lax.fori_loop(0, per_block, turn_passage, 0)
 
-    head = pl.ds(0, flat - tokens)
     lane = lax.broadcasted_iota(jnp.int32, (flat, LANES), 1)
     query_of = lax.broadcasted_iota(jnp.int32, (flat, LANES), 0) // tokens
     my_scores = jnp.zeros((per_block, LANES), jnp.float32)
@@ -180,8 +213,27 @@
     def my_block(slot):
         return table_s[2, me * cap + slot]
 
+    early = products.shape[0]
+
+    def product(slot, block, c, here):
+        passage = p_turned[block, c]
+        return jnp.dot(
+            passage, high[slot, c, :, here], preferred_element_type=jnp.float32
+        ) + jnp.dot(passage, low[slot, c, :, here], preferred_element_type=jnp.float32)
+
+    def early_products(slot, _):
+        block = my_block(slot)
+        for c in range(per_block):
+            for start in range(0, flat, chunk):
+                here = pl.ds(start, chunk)
+                products[slot, c, :, here] = product(slot, block, c, here)
+        return 0
+
     def forward(slot, my_scores):
-        pltpu.make_async_copy(q_slot.at[slot, head], q_slot.at[slot, head], q_sem.at[slot]).wait()
+        @pl.when(lax.rem(slot, q_group) == 0)
+        def _():
+            q_wait(slot // q_group, q_sem.at[slot // q_group])
+
         block = my_block(slot)
         q_turned[slot] = q_slot[slot].T
 
@@ -200,6 +252,10 @@
                 )
                 totals[slot, c : c + 1, here] = jnp.sum(exponent, 0, keepdims=True)
         soft_max = softness * jnp.log(totals[slot])
+        @pl.when(slot == 0)
+        def _():
+            early_products(0, 0)
+
         place = (query_of + slot * rows == lane).astype(jnp.float32)
         return my_scores + jnp.dot(
             soft_max, place, precision=HIGHEST, preferred_element_type=jnp.float32
@@ -220,23 +276,7 @@
         return 0
 
     lax.fori_loop(1, rows, send_scores, 0)
-    early = products.shape[0]
-
-    def product(slot, block, c, here):
-        passage = p_turned[block, c]
-        return jnp.dot(
-            passage, high[slot, c, :, here], preferred_element_type=jnp.float32
-        ) + jnp.dot(passage, low[slot, c, :, here], preferred_element_type=jnp.float32)
-
-    def early_products(slot, _):
-        block = my_block(slot)
-        for c in range(per_block):
-            for start in range(0, flat, chunk):
-                here = pl.ds(start, chunk)
-                products[slot, c, :, here] = product(slot, block, c, here)
-        return 0
-
-    lax.fori_loop(0, early, early_products, 0)
+    lax.fori_loop(1, early, early_products, 0)
     others = pl.ds(0, rows - 1)
     pltpu.make_async_copy(scores.at[others], scores.at[others], score_sem).wait()
 
@@ -276,20 +316,22 @@
         totals[slot] = wide / totals[slot]
         return 0
 
-    lax.fori_loop(0, cap, factors, 0)
+    lax.fori_loop(0, cap, factors, 0, unroll=True)
 
     plus, minus = ring // 2, ring - 1 - ring // 2
     chains = []
     first = 0
-    for half, sign, length in ((0, 1, plus), (0, -1, minus), (1, 1, minus), (1, -1, plus)):
-        chains.append((half, sign, length, first))
-        first += length
+    for local in range(blocks_here):
+        kind = "A" if local < blocks_here // 2 else "B"
+        for sign, length in ((1, plus), (-1, minus)) if kind == "A" else ((1, minus), (-1, plus)):
+            chains.append((local, sign, length, first, kind + ("+" if sign > 0 else "-")))
+            first += length
     order = [
         ring // 2 - (k + 1) // 2 if k % 2 == 1 else k // 2 + ring // 2 for k in range(ring)
     ]
 
     def z_copy(chain, step):
-        half, sign, length, first = chain
+        _, sign, length, first, _ = chain
         return pltpu.make_async_remote_copy(
             src_ref=z_out.at[first + step],
             dst_ref=z_in.at[first + step],
@@ -299,30 +341,33 @@
             device_id_type=MESH,
         )
 
-    def own_part(half):
-        part = acc[pl.ds(half * half_blocks, half_blocks)]
-        return part.reshape(groups, GROUP, width)
+    def ready(chain, hop):
+        _, sign, length, _, _ = chain
+        return [offset % ring for offset in order].index(sign * (length - hop) % ring)
+
+    def own_part(local, step):
+        return acc[step % ACC_SLOTS, local].reshape(groups, GROUP, width)
 
     def z_received(chain, step):
         z_copy(chain, step).wait_recv()
         place = chain[3] + step
-        codes = z_in[place, pl.ds(0, values_here)].astype(jnp.int32).astype(jnp.float32)
-        scale_code = z_in[place, pl.ds(values_here, CODE_ROWS)].astype(jnp.int32)
+        codes = z_in[place, pl.ds(0, passage_len)].astype(jnp.int32).astype(jnp.float32)
+        scale_code = z_in[place, pl.ds(passage_len, CODE_ROWS)].astype(jnp.int32)
         scale = scale_of(scale_code.astype(jnp.float32)[:groups])
         return codes.reshape(groups, GROUP, width) * scale[:, None, :]
 
     def z_hop(chain, step):
-        part = own_part(chain[0])
+        part = own_part(chain[0], ready(chain, step))
         if step:
             part = part + z_received(chain, step - 1)
         codes, scale_code = to_codes(part)
         place = chain[3] + step
-        z_out[place, pl.ds(0, values_here)] = codes.reshape(values_here, width)
+        z_out[place, pl.ds(0, passage_len)] = codes.reshape(passage_len, width)
         if groups < CODE_ROWS:
             scale_code = jnp.concatenate(
                 [scale_code, jnp.zeros((CODE_ROWS - groups, width), jnp.float32)], 0
             )
-        z_out[place, pl.ds(values_here, CODE_ROWS)] = scale_code.astype(jnp.int32).astype(
+        z_out[place, pl.ds(passage_len, CODE_ROWS)] = scale_code.astype(jnp.int32).astype(
             jnp.int16
         )
         z_copy(chain, step).start()
@@ -418,61 +463,64 @@
                 chosen = jnp.where(my_block(slot) == local, 1.0, 0.0)
                 sums[local] = sums[local] + chosen * passage_grad
         for local in range(blocks_here):
-            acc[local] = sums[local]
-        for k in range(per_block):
-
-            @pl.when(step == k)
-            def _(k=k):
-                for chain in chains:
-                    half, sign, length, first = chain
-                    for hop in range(length):
-                        if (sign * (length - hop) - order[k]) % ring == 0:
-                            z_hop(chain, hop)
-
-        @pl.when(step == 0)
-        def _():
-            lax.fori_loop(0, early, early_gradient, 0)
-            start_back(0)
-
-        @pl.when((step > 0) & (step <= cap - early))
-        def _():
-            late_gradient(early + step - 1, 0)
-
-        @pl.when(step == cap - early)
-        def _():
-            start_back(1)
-
-        return 0
+            acc[step % ACC_SLOTS, local] = sums[local]
+
+        for k, actions in enumerate(SCHEDULES[ring]):
+            if actions:
+
+                @pl.when(step == k)
+                def _(actions=actions):
+                    for action in actions:
+                        act(action)
+
+        return 0
+
+    def act(action):
+        kind, number = action[:-1], int(action[-1])
+        if kind == "e":
+            early_gradient(number, 0)
+        elif kind == "l":
+            late_gradient(number, 0)
+        elif kind == "k":
+            start_back(number)
+        else:
+            for chain in chains:
+                if chain[4] == kind:
+                    z_hop(chain, number)
 
     lax.fori_loop(0, per_block, gradients, 0)
 
-    def loss_row(block_row, losses):
-        first = scores_of(place_of(block_row))
-        second = scores_of(place_of(row_blocks + block_row))
-        log_total = jnp.log(
-            jnp.sum(jnp.exp(first), 0, keepdims=True) + jnp.sum(jnp.exp(second), 0, keepdims=True)
-        )
-        positive = positives(block_row)
-        chosen = jnp.sum(jnp.where(column == positive, first, 0.0), 0, keepdims=True) + jnp.sum(
-            jnp.where(column + per_block == positive, second, 0.0), 0, keepdims=True
-        )
-        here = lax.broadcasted_iota(jnp.int32, (1, rows), 1) == me
-        loss = jnp.sum(jnp.where(here, log_total - chosen, 0.0), 1, keepdims=True)
-        return jnp.where(loss_lane == block_row, loss, losses)
-
-    loss_lane = lax.broadcasted_iota(jnp.int32, (1, row_blocks), 1)
-    loss_ref[...] = lax.fori_loop(
-        0, row_blocks, loss_row, jnp.zeros((1, row_blocks), jnp.float32)
-    )
-
-    for half in range(2):
-        result = own_part(half)
+    lane_at = lax.broadcasted_iota(jnp.int32, (per_block, LANES), 1)
+    request_lane = lax.broadcasted_iota(jnp.int32, (per_block, 2 * row_blocks), 1)
+    logits = jnp.zeros((per_block, 2 * row_blocks), jnp.float32)
+    for request in range(2 * row_blocks):
+        place = place_of(request)
+        mine = lane_at == (place % cap) * rows + me
+        value = jnp.sum(jnp.where(mine, scores[place // cap], 0.0), 1, keepdims=True)
+        logits = jnp.where(request_lane == request, value, logits)
+    first, second = logits[:, :row_blocks], logits[:, row_blocks:]
+    log_total = jnp.log(
+        jnp.sum(jnp.exp(first), 0, keepdims=True) + jnp.sum(jnp.exp(second), 0, keepdims=True)
+    )
+    square = (row_blocks, row_blocks)
+    diagonal = lax.broadcasted_iota(jnp.int32, square, 0) == lax.broadcasted_iota(
+        jnp.int32, square, 1
+    )
+    my_column = lax.broadcasted_iota(jnp.int32, pos_ref.shape, 1) == me
+    positive = jnp.sum(jnp.where(my_column, pos_ref[...], 0), 1, keepdims=True)
+    positive = jnp.sum(jnp.where(diagonal, positive, 0), 0, keepdims=True)
+    candidate = lax.broadcasted_iota(jnp.int32, (per_block, row_blocks), 0)
+    chosen = jnp.where(candidate == positive, first, 0.0) + jnp.where(
+        candidate + per_block == positive, second, 0.0
+    )
+    loss_ref[...] = log_total - jnp.sum(chosen, 0, keepdims=True)
+
+    for local in range(blocks_here):
+        result = own_part(local, per_block - 1)
         for chain in chains:
-            if chain[0] == half and chain[2]:
+            if chain[0] == local and chain[2]:
                 result = result + z_received(chain, chain[2] - 1)
-        passage_out[pl.ds(half * half_blocks, half_blocks)] = result.reshape(
-            half_blocks, passage_len, width
-        )
+        passage_out[local] = result.reshape(passage_len, width)
 
     for group in range(2):
         back_others = back_in.at[group, others]
@@ -495,8 +543,8 @@
 
     lax.fori_loop(0, row_blocks, add_pair, 0)
 
-    for slot in range(cap):
-        pltpu.make_async_copy(q_slot.at[slot, head], q_slot.at[slot, head], send_sem.at[0]).wait()
+    for group in range(cap // q_group):
+        q_wait(group, send_sem.at[0])
     pltpu.make_async_copy(scores.at[others], scores.at[others], send_sem.at[1]).wait()
     for group in range(2):
         back_others = back_in.at[group, others]
@@ -518,15 +566,14 @@
     cap = 4 * ((requests + rows - 1) // rows)
     flat = rows * tokens
     vmem = pl.BlockSpec(memory_space=pltpu.VMEM)
-    half_blocks = blocks_here // 2
-    hops = 2 * (ring - 1)
+    hops = blocks_here * (ring - 1)
     f32, bf16, i16 = jnp.float32, jnp.bfloat16, jnp.int16
     out_shape = (
         jax.ShapeDtypeStruct((1, row_blocks), f32),
         jax.ShapeDtypeStruct((row_blocks, tokens, width), f32),
         jax.ShapeDtypeStruct((blocks_here, passage_len, width), f32),
     )
-    z_rows = half_blocks * passage_len + CODE_ROWS
+    z_rows = passage_len + CODE_ROWS
     back_tiles = cap // 2 * tokens // CODE_ROWS + 1
     results = pl.pallas_call(
         functools.partial(main_kernel, rows, ring, cap),
@@ -536,7 +583,7 @@
         scratch_shapes=[
             pltpu.VMEM((8, LANES), jnp.int32),
             pltpu.SMEM((8, LANES), jnp.int32),
-            pltpu.VMEM((cap, rows, tokens, width), bf16),
+            pltpu.VMEM((cap // Q_GROUP, rows, Q_GROUP, tokens, width), bf16),
             pltpu.VMEM((cap, flat, width), bf16),
             pltpu.VMEM((cap, width, flat), bf16),
             pltpu.VMEM((blocks_here, per_block, width, passage_len), bf16),
@@ -551,12 +598,12 @@
             pltpu.VMEM((cap, rows, width), f32),
             pltpu.VMEM((2, rows, back_tiles, CODE_ROWS, width), i16),
             pltpu.VMEM((2, rows, back_tiles, CODE_ROWS, width), i16),
-            pltpu.VMEM((blocks_here, passage_len, width), f32),
+            pltpu.VMEM((ACC_SLOTS, blocks_here, passage_len, width), f32),
             pltpu.VMEM((hops, z_rows, width), i16),
             pltpu.VMEM((hops, z_rows, width), i16),
             pltpu.SemaphoreType.DMA,
             pltpu.SemaphoreType.DMA((4,)),
-            pltpu.SemaphoreType.DMA((cap,)),
+            pltpu.SemaphoreType.DMA((cap // Q_GROUP,)),
             pltpu.SemaphoreType.DMA,
             pltpu.SemaphoreType.DMA((2,)),
             pltpu.SemaphoreType.DMA((hops,)),
@@ -567,7 +614,7 @@
         ),
         name="late_interaction",
     )(
-        cand_ids,
+        cand_ids.T,
         queries.reshape(row_blocks, tokens, width),
         passages,
         pos_index,

time: 72.8 us -> 68.7 us (0.944)
  Pallas kernels: 70.5 us -> 67.9 us
  local copies, waits for them, and re-layouts: 1.35 us -> 0 us
    pallas_call x1, Pallas kernels: 68.5 us -> 65.9 us  [on_device(): pl.pallas_call(functools.partial(main_kernel, rows, ring, cap), out_shape...]
    unnamed x1 -> x0, local copies, waits for them, and re-layouts: 1.35 us -> none
where the time goes in v4:
time: 68.7 us; the launch traced here: 68.6 us
  Pallas kernels  67.9 us (99%)
    pallas_call x1, Pallas kernels, on_device(): pl.pallas_call(functools.partial(main_kernel, rows, ring, cap), out_shape...  65.9 us
    pallas_call x1, Pallas kernels, on_device(): pl.pallas_call(finish_kernel, out_shape=out_shape, in_specs=[vmem] * 3, o...  2.03 us

profile of v4, /device:TPU:1, one launch (start us, length us, event | category | flops | bytes accessed | tf_op | source)
XLA Modules:
  0.0 68.6 jit_solution(7394284867984082830)
XLA Ops:
  0.6 65.9 %late_interaction.1 = (f32[1,16]{1,0:T(1,128)}, f32[16,32,128]{2,1,0:T(8,128)}, f32[4,256,128]{2,1,0:T(8,128)}) custom-call(s32[2,16]{1,0:T(2,128)} %bitcast.10, bf16[16,32,128]{2,1,0:T(8,128)(2,1)} %bitcast.9, bf16[4,8,256,128]{3,2,1,0:T(8,128)(2,1)} %p_ref.1, s32[16,32]{1,0:T(8,128)} %pos_ref.1), custom_call_target="tpu_custom_call" | custom-call | tf_op jit(solution)/shard_map/late_interaction/pallas_call | solution.py:578
  66.5 2.0 %results.1 = (f32[1,16]{1,0:T(1,128)}, f32[16,32,128]{2,1,0:T(8,128)}, f32[4,256,128]{2,1,0:T(8,128)}) custom-call(f32[1,16]{1,0:T(1,128)} %get-tuple-element.9.refs_0_, f32[16,32,128]{2,1,0:T(8,128)} %get-tuple-element.10.refs_1_, f32[4,256,128]{2,1,0:T(8,128)} %get-tuple-element.11.refs_2_), custom_call_target="tpu_custom_call" | custom-call | tf_op jit(solution)/shard_map/results/pallas_call | solution.py:622

commit v5 on v4

--- a/solution.py
+++ b/solution.py
@@ -21,13 +21,13 @@
 GROUP = 32
 CHUNK = 256
 Q_GROUP = 1
-ACC_SLOTS = 4
+ACC_SLOTS = 3
 SCHEDULES = {
     8: (
-        ("A+0", "B-0", "e0"),
-        ("B+0", "e1", "k0"),
-        ("A-0", "A+1", "B-1"),
-        ("l2",),
+        ("A+0", "B-0"),
+        ("B+0", "e0"),
+        ("A-0", "e1", "k0", "A+1", "B-1"),
+        ("e2",),
         ("B+1", "A-1"),
         ("l3", "k1", "A+2", "B-2"),
         ("B+2", "A-2", "A+3", "B-3"),
@@ -333,7 +333,7 @@
     def z_copy(chain, step):
         _, sign, length, first, _ = chain
         return pltpu.make_async_remote_copy(
-            src_ref=z_out.at[first + step],
+            src_ref=z_in.at[first + step - 1] if step else z_out.at[chains.index(chain)],
             dst_ref=z_in.at[first + step],
             send_sem=z_send_sem.at[first + step],
             recv_sem=z_recv_sem.at[first + step],
@@ -361,13 +361,13 @@
         if step:
             part = part + z_received(chain, step - 1)
         codes, scale_code = to_codes(part)
-        place = chain[3] + step
-        z_out[place, pl.ds(0, passage_len)] = codes.reshape(passage_len, width)
+        message = z_in.at[chain[3] + step - 1] if step else z_out.at[chains.index(chain)]
+        message[pl.ds(0, passage_len)] = codes.reshape(passage_len, width)
         if groups < CODE_ROWS:
             scale_code = jnp.concatenate(
                 [scale_code, jnp.zeros((CODE_ROWS - groups, width), jnp.float32)], 0
             )
-        z_out[place, pl.ds(passage_len, CODE_ROWS)] = scale_code.astype(jnp.int32).astype(
+        message[pl.ds(passage_len, CODE_ROWS)] = scale_code.astype(jnp.int32).astype(
             jnp.int16
         )
         z_copy(chain, step).start()
@@ -591,7 +591,7 @@
             pltpu.VMEM((cap, per_block, passage_len, flat), bf16),
             pltpu.VMEM((cap, per_block, flat), f32),
             pltpu.VMEM((rows, per_block, LANES), f32),
-            pltpu.VMEM((cap // 2, per_block, width, flat), f32),
+            pltpu.VMEM((cap // 2 + 1, per_block, width, flat), f32),
             pltpu.VMEM((2 * width, flat), bf16),
             pltpu.VMEM((2 * width, flat), bf16),
             pltpu.VMEM((width, flat), f32),
@@ -599,7 +599,7 @@
             pltpu.VMEM((2, rows, back_tiles, CODE_ROWS, width), i16),
             pltpu.VMEM((2, rows, back_tiles, CODE_ROWS, width), i16),
             pltpu.VMEM((ACC_SLOTS, blocks_here, passage_len, width), f32),
-            pltpu.VMEM((hops, z_rows, width), i16),
+            pltpu.VMEM((2 * blocks_here, z_rows, width), i16),
             pltpu.VMEM((hops, z_rows, width), i16),
             pltpu.SemaphoreType.DMA,
             pltpu.SemaphoreType.DMA((4,)),
@@ -610,7 +610,7 @@
             pltpu.SemaphoreType.DMA((hops,)),
         ],
         compiler_params=pltpu.CompilerParams(
-            collective_id=0, has_side_effects=True, vmem_limit_bytes=62 * 1024 * 1024
+            collective_id=0, has_side_effects=True, vmem_limit_bytes=63 * 1024 * 1024
         ),
         name="late_interaction",
     )(

time: 68.7 us -> 67.6 us (0.984)
  Pallas kernels: 67.9 us -> 66.8 us
    pallas_call x1, Pallas kernels: 65.9 us -> 64.7 us  [on_device(): pl.pallas_call(functools.partial(main_kernel, rows, ring, cap), out_shape...]
where the time goes in v5:
time: 67.6 us; the launch traced here: 67.4 us
  Pallas kernels  66.8 us (99%)
    pallas_call x1, Pallas kernels, on_device(): pl.pallas_call(functools.partial(main_kernel, rows, ring, cap), out_shape...  64.7 us
    pallas_call x1, Pallas kernels, on_device(): pl.pallas_call(finish_kernel, out_shape=out_shape, in_specs=[vmem] * 3, o...  2.03 us

profile of v5, /device:TPU:1, one launch (start us, length us, event | category | flops | bytes accessed | tf_op | source)
XLA Modules:
  0.0 67.4 jit_solution(14787745298906062008)
XLA Ops:
  0.6 64.7 %late_interaction.1 = (f32[1,16]{1,0:T(1,128)}, f32[16,32,128]{2,1,0:T(8,128)}, f32[4,256,128]{2,1,0:T(8,128)}) custom-call(s32[2,16]{1,0:T(2,128)} %bitcast.10, bf16[16,32,128]{2,1,0:T(8,128)(2,1)} %bitcast.9, bf16[4,8,256,128]{3,2,1,0:T(8,128)(2,1)} %p_ref.1, s32[16,32]{1,0:T(8,128)} %pos_ref.1), custom_call_target="tpu_custom_call" | custom-call | tf_op jit(solution)/shard_map/late_interaction/pallas_call | solution.py:578
  65.4 2.0 %results.1 = (f32[1,16]{1,0:T(1,128)}, f32[16,32,128]{2,1,0:T(8,128)}, f32[4,256,128]{2,1,0:T(8,128)}) custom-call(f32[1,16]{1,0:T(1,128)} %get-tuple-element.9.refs_0_, f32[16,32,128]{2,1,0:T(8,128)} %get-tuple-element.10.refs_1_, f32[4,256,128]{2,1,0:T(8,128)} %get-tuple-element.11.refs_2_), custom_call_target="tpu_custom_call" | custom-call | tf_op jit(solution)/shard_map/results/pallas_call | solution.py:622

commit v6 on v5

--- a/solution.py
+++ b/solution.py
@@ -515,13 +515,6 @@
     )
     loss_ref[...] = log_total - jnp.sum(chosen, 0, keepdims=True)
 
-    for local in range(blocks_here):
-        result = own_part(local, per_block - 1)
-        for chain in chains:
-            if chain[0] == local and chain[2]:
-                result = result + z_received(chain, chain[2] - 1)
-        passage_out[local] = result.reshape(passage_len, width)
-
     for group in range(2):
         back_others = back_in.at[group, others]
         pltpu.make_async_copy(back_others, back_others, back_sem.at[group]).wait()
@@ -541,7 +534,14 @@
         query_out[block_row] = piece(place_of(block_row)) + piece(second)
         return 0
 
-    lax.fori_loop(0, row_blocks, add_pair, 0)
+    lax.fori_loop(0, row_blocks, add_pair, 0, unroll=4)
+
+    for local in range(blocks_here):
+        result = own_part(local, per_block - 1)
+        for chain in chains:
+            if chain[0] == local and chain[2]:
+                result = result + z_received(chain, chain[2] - 1)
+        passage_out[local] = result.reshape(passage_len, width)
 
     for group in range(cap // q_group):
         q_wait(group, send_sem.at[0])

time: 67.6 us -> 67.4 us (level)
  no operation moved by 1% of the time
where the time goes in v6:
time: 67.4 us; the launch traced here: 67.3 us
  Pallas kernels  66.7 us (99%)
    pallas_call x1, Pallas kernels, on_device(): pl.pallas_call(functools.partial(main_kernel, rows, ring, cap), out_shape...  64.6 us
    pallas_call x1, Pallas kernels, on_device(): pl.pallas_call(finish_kernel, out_shape=out_shape, in_specs=[vmem] * 3, o...  2.03 us

profile of v6, /device:TPU:1, one launch (start us, length us, event | category | flops | bytes accessed | tf_op | source)
XLA Modules:
  0.0 67.3 jit_solution(7994785247482703621)
XLA Ops:
  0.6 64.6 %late_interaction.1 = (f32[1,16]{1,0:T(1,128)}, f32[16,32,128]{2,1,0:T(8,128)}, f32[4,256,128]{2,1,0:T(8,128)}) custom-call(s32[2,16]{1,0:T(2,128)} %bitcast.10, bf16[16,32,128]{2,1,0:T(8,128)(2,1)} %bitcast.9, bf16[4,8,256,128]{3,2,1,0:T(8,128)(2,1)} %p_ref.1, s32[16,32]{1,0:T(8,128)} %pos_ref.1), custom_call_target="tpu_custom_call" | custom-call | tf_op jit(solution)/shard_map/late_interaction/pallas_call | solution.py:578
  65.3 2.0 %results.1 = (f32[1,16]{1,0:T(1,128)}, f32[16,32,128]{2,1,0:T(8,128)}, f32[4,256,128]{2,1,0:T(8,128)}) custom-call(f32[1,16]{1,0:T(1,128)} %get-tuple-element.9.refs_0_, f32[16,32,128]{2,1,0:T(8,128)} %get-tuple-element.10.refs_1_, f32[4,256,128]{2,1,0:T(8,128)} %get-tuple-element.11.refs_2_), custom_call_target="tpu_custom_call" | custom-call | tf_op jit(solution)/shard_map/results/pallas_call | solution.py:622
